TPU v7x, 32 devices: a whole 2x2x4 slice. The times are simulated.
32 devices in a mesh: row: 8 (over z, core), col: 4 (over y, x).
Axes of the slice: x: 2, y: 2, z: 4, core: 2. Of those that a mesh axis runs over, the one named last changes fastest.
Arguments:
- inv_diag: bfloat16 [4, 8192, 8192], P(None, 'col', 'row'), as said below
- off_diag: bfloat16 [4, 1792, 8192], P(None, 'row', 'col'), may hold values from -0.0625 to 0.0625
- rhs: bfloat16 [4, 8192, 768], P(None, 'row'), may hold values from -6 to 6
- anc_rhs: float32 [1792, 768], P('row'), may hold values from -12 to 12
- dest_device: int32 [56, 4, 1], replicated, may hold values from 0 to 7, as said below
- dest_slot: int32 [56, 4], replicated, may hold values from 0 to 6
Outputs:
- solution: bfloat16 [4, 8192, 768], P(None, ('col', 'row'))
- anc_out: float32 [1792, 768], P('row')
Inputs may be any that keep to these rules, and one draw needn't show every extreme that they name: inv_diag[s] is zero above its diagonal. Within one supernode s, distinct row blocks j belong to distinct ancestor blocks. Among the 28 entries dest_device[j, s] with j in one index of row's range of 7 blocks, every value occurs either 0 or exactly 7 times.
All inputs are finite; a program needn't handle non-finite values.
Results may differ from a plain program's by a relative error of at most 0.014.
Values may be sent and summed in bfloat16 or wider, within the bound.
No kernel may reach another device: no remote copies, remote signals or barrier semaphores. Data moves between devices by JAX's collectives and lax.ppermute only.
A program may use at most 128 MiB of HBM per device.

v0:
```python
import functools

import jax
import jax.numpy as jnp
from jax import lax
from jax.experimental import pallas as pl
from jax.experimental.pallas import tpu as pltpu
from jax.sharding import PartitionSpec as P

SNODES = 4
BLOCK = 32
HALVES = 2
AHEAD = 4
STREAMS = 2
F32 = jnp.float32
BF16 = jnp.bfloat16


def add16(*terms):
    return functools.reduce(lambda a, b: a + b, [t.astype(F32) for t in terms]).astype(BF16)


def pick(array, index, axis):
    return lax.dynamic_index_in_dim(array, index, axis, keepdims=False)


def after(value, *earlier):
    return lax.optimization_barrier((value,) + earlier)[0]


def product_kernel(first, meta_ref, tile_ref, rhs_ref, *refs):
    outs, (tile, part, terms, tile_sem, part_sem, out_sem) = refs[:-6], refs[-6:]
    per, nz = tile.shape[:2]
    z, side = meta_ref[0], meta_ref[1]
    width = terms.shape[-1]
    reads = []
    for s in range(per):
        reads.append([pltpu.make_async_copy(rhs_ref.at[first + s], part.at[s], part_sem.at[s])])
        for d in range(nz):
            reads[s].append(pltpu.make_async_copy(tile_ref.at[first + s, d], tile.at[s, d], tile_sem.at[s, d]))
    queue = [copy for copies in reads for copy in copies]
    for copy in queue[:AHEAD]:
        copy.start()
    queue = queue[AHEAD:]

    def await_next(copy):
        copy.wait()
        if queue:
            queue.pop(0).start()

    writes = []
    for s in range(per):
        await_next(reads[s][0])
        for d in range(nz):
            await_next(reads[s][d + 1])
            both = jnp.dot(tile[s, d], part[s], preferred_element_type=F32).astype(BF16)
            place = (d - z) * side
            for n in range(HALVES):
                terms[s, d, n] = both[:, n * width : (n + 1) * width]
                source, sem = terms.at[s, d, n], out_sem.at[s, d, n]
                away = pltpu.make_async_copy(source, outs[2 * n].at[jnp.clip(-1 - place, 0, nz - 2), s], sem)
                keep = pltpu.make_async_copy(source, outs[2 * n + 1].at[jnp.clip(place, 0, nz - 1), s], sem)
                pl.when(place < 0)(away.start)
                pl.when(place >= 0)(keep.start)
                writes.append((place, away, keep))
    for place, away, keep in writes:
        pl.when(place < 0)(away.wait)
        pl.when(place >= 0)(keep.wait)


def apply_product(meta, tiles, rhs, first, per):
    nz, rows, depth = tiles.shape[1:]
    width = rhs.shape[2] // HALVES
    hbm = pl.BlockSpec(memory_space=pl.ANY)
    outs = pl.pallas_call(
        functools.partial(product_kernel, first),
        in_specs=[pl.BlockSpec(memory_space=pltpu.SMEM), hbm, hbm],
        out_specs=[hbm] * (2 * HALVES),
        out_shape=[
            jax.ShapeDtypeStruct((nz - 1, per, rows, width), BF16),
            jax.ShapeDtypeStruct((nz, per, rows, width), BF16),
        ]
        * HALVES,
        scratch_shapes=[
            pltpu.VMEM((per, nz, rows, depth), BF16),
            pltpu.VMEM((per, depth, rhs.shape[2]), BF16),
            pltpu.VMEM((per, nz, HALVES, rows, width), BF16),
            pltpu.SemaphoreType.DMA((per, nz)),
            pltpu.SemaphoreType.DMA((per,)),
            pltpu.SemaphoreType.DMA((per, nz, HALVES)),
        ],
        compiler_params=pltpu.CompilerParams(vmem_limit_bytes=56 * 1024 * 1024),
        cost_estimate=pl.CostEstimate(
            flops=2 * per * nz * rows * depth * rhs.shape[2],
            bytes_accessed=2 * per * (nz * rows * (depth + rhs.shape[2]) + depth * rhs.shape[2]),
            transcendentals=0,
        ),
    )(meta, tiles, rhs)
    return [outs[2 * n : 2 * n + 2] for n in range(HALVES)]


def update_kernel(places, has_base, table_ref, meta_ref, mine_ref, theirs_ref, *refs):
    ends = 2 * has_base + STREAMS * len(places)
    sources, scratch = refs[2 * has_base : ends], refs[ends:]
    out_ref, total, part, rows_both, pieces, sem, piece_sem = scratch[:7]
    per, rows = sources[0].shape[:2]
    z, side, last = meta_ref[0], meta_ref[1], meta_ref[2]
    core = (1 - side) // 2
    upstream = jnp.where(core == 0, z, last - z)
    height = part.shape[0] // 2
    blocks = 2 * height // BLOCK
    half = rows // 2
    raw = len(mine_ref.shape) == 3
    only = places[0] if len(places) == 1 else None
    reach = upstream >= places[0]
    if has_base:
        base = pltpu.make_async_copy(refs[0], scratch[7], scratch[8])
        base.start()
        after_ref, next_rows, next_sem = refs[1], scratch[9], scratch[10]
        extend = upstream == places[0]
        nexts = [pltpu.make_async_copy(after_ref.at[s], next_rows.at[s], next_sem.at[s]) for s in range(SNODES)]
    reads, arrive = [], []
    for s in range(SNODES):
        for i, ref in enumerate((mine_ref, theirs_ref)):
            chip = jnp.clip(z - side * places[0], 0, last)
            if only is not None and raw:
                source = ref.at[s, :, pl.ds(pl.multiple_of(chip * rows, rows), rows)]
                spot = rows_both.at[s, pl.ds(i * height, height), pl.ds(0, rows)]
            elif raw:
                source, spot = ref.at[s], rows_both.at[s, pl.ds(i * height, height)]
            else:
                source, spot = ref.at[s], rows_both.at[s, :, pl.ds(i * height, height)]
            reads.append(pltpu.make_async_copy(source, spot, sem.at[s, i]))
            pl.when(reach)(reads[-1].start)
        if has_base:
            pl.when(extend)(nexts[s].start)
        if s % per == 0:
            for i, t in enumerate(places):
                k = (s // per) * len(places) + i
                arrive.append(pltpu.make_async_copy(sources[k], pieces.at[k], piece_sem.at[k]))
                pl.when(upstream >= t)(arrive[-1].start)

    def factor(s, start, count):
        if only is not None and raw:
            return rows_both[s, :, :rows]
        if raw:
            return rows_both[s, :, pl.ds(pl.multiple_of(start * count, count), count)]
        both = rows_both[s, start // (rows // count)]
        return both if count == rows else jnp.where(core == 0, both[:, :count], both[:, count:])

    if has_base:
        base.wait()
        total[...] = scratch[7][...].astype(F32)
    else:
        total[...] = jnp.zeros_like(total)

    @pl.when(reach)
    def _():
        for s in range(SNODES):
            reads[2 * s].wait()
            reads[2 * s + 1].wait()
            first = (s // per) * len(places)
            if s % per == 0:
                for i, t in enumerate(places):
                    pl.when(upstream >= t)(arrive[first + i].wait)
            for i, t in enumerate(places):
                if t == 0:
                    part[...] = jnp.dot(
                        factor(s, 2 * z + core, half),
                        pieces[first, s % per, pl.ds(pl.multiple_of(core * half, half), half)],
                        preferred_element_type=F32,
                    )
                    continue
                chip = jnp.clip(z - side * t, 0, last)
                if i == 0:
                    part[...] = jnp.dot(
                        factor(s, chip, rows), pieces[first, s % per], preferred_element_type=F32
                    )
                    continue

                @pl.when(upstream >= t)
                def _():
                    part[...] += jnp.dot(
                        factor(s, chip, rows), pieces[first + i, s % per], preferred_element_type=F32
                    )

            for b in range(blocks):
                total[table_ref[s * blocks + b]] += part[b * BLOCK : (b + 1) * BLOCK]
            if has_base:

                @pl.when(extend)
                def _():
                    nexts[s].wait()
                    part[...] = jnp.dot(next_rows[s], pieces[first, s % per], preferred_element_type=F32)
                    for b in range(blocks):
                        total[table_ref[(SNODES + s) * blocks + b]] += part[b * BLOCK : (b + 1) * BLOCK]

    out_ref[...] = total[...].astype(out_ref.dtype)


def apply_update(table, meta, mine, theirs, got, places, anc_blocks, *extra):
    pieces = [x[t] for x in got for t in places]
    width = pieces[0].shape[-1]
    height = mine.shape[-2]
    hbm = pl.BlockSpec(memory_space=pl.ANY)
    both = list(mine.shape)
    both[-2] *= 2
    if mine.ndim == 3 and len(places) == 1:
        both[-1] = pieces[0].shape[-2]
    block = (anc_blocks, BLOCK, width)
    has_base = len(extra) // 2
    return pl.pallas_call(
        functools.partial(update_kernel, places, has_base),
        out_shape=jax.ShapeDtypeStruct(block, BF16),
        in_specs=[pl.BlockSpec(memory_space=pltpu.SMEM)] * 2 + [hbm] * (2 + len(extra) + len(pieces)),
        out_specs=pl.BlockSpec(memory_space=pltpu.VMEM),
        scratch_shapes=[
            pltpu.VMEM(block, F32),
            pltpu.VMEM((2 * height, width), F32),
            pltpu.VMEM(tuple(both), BF16),
            pltpu.VMEM((len(pieces),) + pieces[0].shape, BF16),
            pltpu.SemaphoreType.DMA((SNODES, 2)),
            pltpu.SemaphoreType.DMA((len(pieces),)),
        ]
        + [
            pltpu.VMEM(block, BF16),
            pltpu.SemaphoreType.DMA,
            pltpu.VMEM((SNODES, 2 * height, pieces[0].shape[-2]), BF16),
            pltpu.SemaphoreType.DMA((SNODES,)),
        ]
        * has_base,
        compiler_params=pltpu.CompilerParams(vmem_limit_bytes=60 * 1024 * 1024),
        cost_estimate=pl.CostEstimate(
            flops=4 * mine.size * width * len(places) // 4,
            bytes_accessed=mine.size * 4 + anc_blocks * BLOCK * width * 2,
            transcendentals=0,
        ),
    )(table, meta, mine, theirs, *extra, *pieces)


def per_device(inv_diag, off_diag, rhs, anc_rhs, dest_device, dest_slot):
    n_row, n_col = lax.axis_size("row"), lax.axis_size("col")
    nz = n_row // 2
    row, col = lax.axis_index("row"), lax.axis_index("col")
    z, core = row // 2, row % 2
    side = 1 - 2 * core
    own_rows = inv_diag.shape[1] // n_row
    anc_dev = anc_rhs.shape[0] // BLOCK
    anc_blocks = n_row * anc_dev
    width = rhs.shape[2] // HALVES
    per = SNODES // STREAMS
    pair = [(r, r ^ 1) for r in range(n_row)]

    def hop(value, sources):
        up = [(2 * i, 2 * i + 2) for i in sources if i + 1 < nz]
        down = [(2 * (nz - 1 - i) + 1, 2 * (nz - 2 - i) + 1) for i in sources if i + 1 < nz]
        return lax.ppermute(value, "row", up + down)

    tiles = inv_diag.reshape(SNODES, nz, 2 * own_rows, inv_diag.shape[2])
    meta = jnp.stack([z, side, jnp.full_like(z, nz - 1)]).astype(jnp.int32)

    def sum_cores(terms):
        away, keep = terms
        other = lax.ppermute(away, "row", pair)
        return [(keep[0],)] + [(keep[j], other[j - 1]) for j in range(1, nz)]

    turns = [[(i, i ^ d) for i in range(n_col)] for d in range(1, n_col)]
    moves = [[(2 * i + q, 2 * ((i + d) % nz) + q) for i in range(nz) for q in range(2)] for d in range(1, nz)]

    def share_cores(total):
        total = total.reshape(nz, 2, anc_dev, n_col, BLOCK // n_col, width)
        return add16(pick(total, core, 1), lax.ppermute(pick(total, 1 - core, 1), "row", pair))

    def share_col(total):
        return add16(
            pick(total, col, 2),
            *[lax.ppermute(pick(total, col ^ d, 2), "col", turns[d - 1]) for d in range(1, n_col)],
        )

    def share_line(total):
        return add16(
            pick(total, z, 0),
            *[lax.ppermute(pick(total, (z + d) % nz, 0), "row", moves[d - 1]) for d in range(1, nz)],
        )

    def share_out(total):
        whole = jnp.zeros((anc_dev, n_col) + total.shape[1:], BF16)
        whole = lax.dynamic_update_index_in_dim(whole, total, col, 1)
        for d in range(1, n_col):
            other = lax.ppermute(total, "col", turns[d - 1])
            whole = lax.dynamic_update_index_in_dim(whole, other, col ^ d, 1)
        return whole.reshape(anc_dev * BLOCK, whole.shape[-1])

    shares = [share_cores, share_col, share_line]

    per_dev = off_diag.shape[1] // BLOCK
    target = (dest_device[:, :, 0] * anc_dev + dest_slot).reshape(n_row, per_dev, SNODES)
    onward = jnp.clip(row + 2 * side, 0, n_row - 1)
    table = jnp.concatenate(
        [
            jnp.concatenate([pick(target, r, 0), pick(target, r ^ 1, 0)], axis=0).T.reshape(-1)
            for r in (row, onward)
        ]
    )
    split = (lambda x: x) if (own_rows % 128 == 0) else (
        lambda x: x.reshape(SNODES, x.shape[1], nz, 2 * own_rows).transpose(0, 2, 1, 3)
    )

    terms, last = [], ()
    for s in range(STREAMS):
        raw = apply_product(after(meta, *last), tiles, rhs, s * per, per)
        last = (raw[0][1],)
        terms.append([sum_cores(x) for x in raw])

    own = [[None] * HALVES for _ in range(STREAMS)]
    upstream = jnp.where(core == 0, z, nz - 1 - z)
    flows = [()] * STREAMS
    for t in range(1, nz):
        for s in range(STREAMS):
            flows[s] = (hop(add16(*terms[s][0][nz - t], *flows[s]), range(t)),)
        if t == 1:
            theirs = lax.ppermute(after(off_diag, flows[0][0]), "row", pair)
    mine, theirs = split(off_diag), split(theirs)

    waiting = None
    for n in range(HALVES):
        partial = [add16(*terms[s][n][0], *flows[s]) for s in range(STREAMS)]
        for s in range(STREAMS):
            own[s][n] = add16(partial[s], lax.ppermute(partial[s], "row", pair))
        got = [[own[s][n]] for s in range(STREAMS)]
        for t in range(1, nz + 1):
            for s in range(STREAMS):
                send = got[s][-1]
                if n + 1 < HALVES:
                    if t > 1:
                        late = functools.reduce(
                            lambda a, b: a + b, [x.astype(F32) for x in terms[s][n + 1][nz - t + 1]]
                        )
                        send = (send.astype(F32) + jnp.where(upstream >= t - 1, 0.0, late)).astype(BF16)
                    got[s].append(hop(send, range(nz)))
                elif t < nz - 1:
                    got[s].append(hop(send, range(t - 1, nz)))
                    if n and s == 0 and t == 1:
                        total = apply_update(
                            table, after(meta, got[0][1]), mine, theirs, before, range(nz), anc_blocks
                        )
        if n + 1 < HALVES:
            flows = [(got[s].pop(),) for s in range(STREAMS)]
        if n:
            waiting = share_col(share_cores(total))
        before = got
    if mine.ndim == 3:
        last_rows = [lax.dynamic_slice_in_dim(x, core * (nz - 1) * 2 * own_rows, 2 * own_rows, 2) for x in (mine, theirs)]
    else:
        last_rows = [pick(x, core * (nz - 1), 1) for x in (mine, theirs)]
    back = lax.ppermute(
        after(jnp.concatenate(last_rows, axis=1), got[0][1]), "row", [(2 * nz - 2, 2 * nz - 4), (1, 3)]
    )
    total = apply_update(table, after(meta, got[0][nz - 2]), mine, theirs, got, range(nz - 2), anc_blocks)
    total = apply_update(table, after(meta, waiting), mine, theirs, got, [nz - 2], anc_blocks, total, back)
    total = jnp.concatenate([waiting, share_col(share_cores(total))], axis=-1)
    update = share_out(share_line(total))
    solution = jnp.concatenate(
        [jnp.concatenate(
                [lax.dynamic_slice_in_dim(own[s][n], core * own_rows, own_rows, 1) for n in range(HALVES)], axis=2
            ) for s in range(STREAMS)],
        axis=0,
    )
    anc_out = anc_rhs - update.astype(F32)
    return (solution, anc_out)


def solution(mesh):
    in_specs = (
        P(None, "col", "row"),
        P(None, "row", "col"),
        P(None, "row", None),
        P("row", None),
        P(),
        P(),
    )
    out_specs = (P(None, ("col", "row"), None), P("row", None))
    return jax.shard_map(
        per_device, mesh=mesh, in_specs=in_specs, out_specs=out_specs, check_vma=False
    )
```

profile of v0, /device:TPU:0, one launch (start us, length us, event | category | flops | bytes accessed | tf_op | source)
XLA Modules:
  0.0 261.0 jit_solution(8202662787501956003)
XLA Ops:
  1.3 13.6 %shard_map.77 = (bf16[3,2,512,384]{3,2,1,0:T(8,128)(2,1)}, bf16[4,2,512,384]{3,2,1,0:T(8,128)(2,1)}, bf16[3,2,512,384]{3,2,1,0:T(8,128)(2,1)}, bf16[4,2,512,384]{3,2,1,0:T(8,128)(2,1)}) custom-call(s32[3]{0:T(128)} %pad_add_fusion.meta_ref, bf16[4,4,512,1024]{3,2,1,0:T(8,128)(2,1)} %bitcast.144, bf16[4,1024,768]{2,1,0:T(8,128)(2,1)} %rhs_ref.3), custom_call_target="tpu_custom_call" | custom-call | flops 6442450944 | bytes 17825792 | tf_op jit(solution)/shard_map/pallas_call | solution.py:75
  15.4 14.1 %shard_map.78 = (bf16[3,2,512,384]{3,2,1,0:T(8,128)(2,1)}, bf16[4,2,512,384]{3,2,1,0:T(8,128)(2,1)}, bf16[3,2,512,384]{3,2,1,0:T(8,128)(2,1)}, bf16[4,2,512,384]{3,2,1,0:T(8,128)(2,1)}) custom-call(s32[3]{0:T(128)} %pad_add_fusion.meta_ref, bf16[4,4,512,1024]{3,2,1,0:T(8,128)(2,1)} %bitcast.145, bf16[4,1024,768]{2,1,0:T(8,128)(2,1)} %rhs_ref.3), custom_call_target="tpu_custom_call" | custom-call | flops 6442450944 | bytes 17825792 | tf_op jit(solution)/shard_map/pallas_call | solution.py:75
  29.9 5.0 %collective-permute-start.1 = (bf16[2,512,384]{2,1,0:T(8,128)(2,1)S(1)}, bf16[2,512,384]{2,1,0:T(8,128)(2,1)S(1)}, u32[]{:S(2)}, u32[]{:S(2)}) collective-permute-start(bf16[2,512,384]{2,1,0:T(8,128)(2,1)S(1)} %fusion.16), channel_id=1, source_target_pairs={{0,8},{28,20},{1,9},{29,21},{2,10},{30,22},{3,11},{31,23}} | collective-permute-start | bytes 2359304 | tf_op jit(solution)/shard_map/ppermute | solution.py:257
  34.9 1.4 fusion.17
  36.2 4.4 %collective-permute-start.12 = (bf16[2,512,384]{2,1,0:T(8,128)(2,1)S(1)}, bf16[2,512,384]{2,1,0:T(8,128)(2,1)S(1)}, u32[]{:S(2)}, u32[]{:S(2)}) collective-permute-start(bf16[2,512,384]{2,1,0:T(8,128)(2,1)S(1)} %fusion.17), channel_id=1, source_target_pairs={{0,8},{28,20},{1,9},{29,21},{2,10},{30,22},{3,11},{31,23}} | collective-permute-start | bytes 2359304 | tf_op jit(solution)/shard_map/ppermute | solution.py:257
  40.7 3.6 %collective-permute-done.1 = bf16[2,512,384]{2,1,0:T(8,128)(2,1)S(1)} collective-permute-done((bf16[2,512,384]{2,1,0:T(8,128)(2,1)S(1)}, bf16[2,512,384]{2,1,0:T(8,128)(2,1)S(1)}, u32[]{:S(2)}, u32[]{:S(2)}) %collective-permute-start.1) | collective-permute-done | bytes 786464 | tf_op jit(solution)/shard_map/ppermute | solution.py:257
  44.6 4.4 %collective-permute-start.2 = (bf16[2,512,384]{2,1,0:T(8,128)(2,1)S(1)}, bf16[2,512,384]{2,1,0:T(8,128)(2,1)S(1)}, u32[]{:S(2)}, u32[]{:S(2)}) collective-permute-start(bf16[2,512,384]{2,1,0:T(8,128)(2,1)S(1)} %fusion.12), channel_id=1, source_target_pairs={{0,8},{8,16},{28,20},{20,12},{1,9},{9,17},{29,21},{21,13},{2,10},{... | collective-permute-start | bytes 2359304 | tf_op jit(solution)/shard_map/ppermute | solution.py:257
  49.1 3.7 %collective-permute-done.12 = bf16[2,512,384]{2,1,0:T(8,128)(2,1)S(1)} collective-permute-done((bf16[2,512,384]{2,1,0:T(8,128)(2,1)S(1)}, bf16[2,512,384]{2,1,0:T(8,128)(2,1)S(1)}, u32[]{:S(2)}, u32[]{:S(2)}) %collective-permute-start.12) | collective-permute-done | bytes 786464 | tf_op jit(solution)/shard_map/ppermute | solution.py:257
  53.1 4.4 %collective-permute-start.13 = (bf16[2,512,384]{2,1,0:T(8,128)(2,1)S(1)}, bf16[2,512,384]{2,1,0:T(8,128)(2,1)S(1)}, u32[]{:S(2)}, u32[]{:S(2)}) collective-permute-start(bf16[2,512,384]{2,1,0:T(8,128)(2,1)S(1)} %fusion.7), channel_id=1, source_target_pairs={{0,8},{8,16},{28,20},{20,12},{1,9},{9,17},{29,21},{21,13},{2,10},{... | collective-permute-start | bytes 2359304 | tf_op jit(solution)/shard_map/ppermute | solution.py:257
  57.5 3.7 %collective-permute-done.2 = bf16[2,512,384]{2,1,0:T(8,128)(2,1)S(1)} collective-permute-done((bf16[2,512,384]{2,1,0:T(8,128)(2,1)S(1)}, bf16[2,512,384]{2,1,0:T(8,128)(2,1)S(1)}, u32[]{:S(2)}, u32[]{:S(2)}) %collective-permute-start.2) | collective-permute-done | bytes 786464 | tf_op jit(solution)/shard_map/ppermute | solution.py:257
  61.5 4.4 %collective-permute-start.3 = (bf16[2,512,384]{2,1,0:T(8,128)(2,1)S(1)}, bf16[2,512,384]{2,1,0:T(8,128)(2,1)S(1)}, u32[]{:S(2)}, u32[]{:S(2)}) collective-permute-start(bf16[2,512,384]{2,1,0:T(8,128)(2,1)S(1)} %fusion.13), channel_id=1, source_target_pairs={{0,8},{8,16},{16,24},{28,20},{20,12},{12,4},{1,9},{9,17},{17,25},{... | collective-permute-start | bytes 2359304 | tf_op jit(solution)/shard_map/ppermute | solution.py:257
  66.0 3.6 %collective-permute-done.13 = bf16[2,512,384]{2,1,0:T(8,128)(2,1)S(1)} collective-permute-done((bf16[2,512,384]{2,1,0:T(8,128)(2,1)S(1)}, bf16[2,512,384]{2,1,0:T(8,128)(2,1)S(1)}, u32[]{:S(2)}, u32[]{:S(2)}) %collective-permute-start.13) | collective-permute-done | bytes 786464 | tf_op jit(solution)/shard_map/ppermute | solution.py:257
  69.9 4.4 %collective-permute-start.14 = (bf16[2,512,384]{2,1,0:T(8,128)(2,1)S(1)}, bf16[2,512,384]{2,1,0:T(8,128)(2,1)S(1)}, u32[]{:S(2)}, u32[]{:S(2)}) collective-permute-start(bf16[2,512,384]{2,1,0:T(8,128)(2,1)S(1)} %fusion.8), channel_id=1, source_target_pairs={{0,8},{8,16},{16,24},{28,20},{20,12},{12,4},{1,9},{9,17},{17,25},{... | collective-permute-start | bytes 2359304 | tf_op jit(solution)/shard_map/ppermute | solution.py:257
  74.4 3.7 %collective-permute-done.3 = bf16[2,512,384]{2,1,0:T(8,128)(2,1)S(1)} collective-permute-done((bf16[2,512,384]{2,1,0:T(8,128)(2,1)S(1)}, bf16[2,512,384]{2,1,0:T(8,128)(2,1)S(1)}, u32[]{:S(2)}, u32[]{:S(2)}) %collective-permute-start.3) | collective-permute-done | bytes 786464 | tf_op jit(solution)/shard_map/ppermute | solution.py:257
  78.8 7.7 %collective-permute-done.14 = bf16[2,512,384]{2,1,0:T(8,128)(2,1)S(1)} collective-permute-done((bf16[2,512,384]{2,1,0:T(8,128)(2,1)S(1)}, bf16[2,512,384]{2,1,0:T(8,128)(2,1)S(1)}, u32[]{:S(2)}, u32[]{:S(2)}) %collective-permute-start.14) | collective-permute-done | bytes 786464 | tf_op jit(solution)/shard_map/ppermute | solution.py:257
  87.0 4.4 %collective-permute-start.5 = (bf16[2,512,384]{2,1,0:T(8,128)(2,1)S(1)}, bf16[2,512,384]{2,1,0:T(8,128)(2,1)S(1)}, u32[]{:S(2)}, u32[]{:S(2)}) collective-permute-start(bf16[2,512,384]{2,1,0:T(8,128)(2,1)S(1)} %add_convert_fusion.4.refs_0_), channel_id=1, source_target_pairs={{0,8},{8,16},{16,24},{28,20},{20,12},{12,4},{1,9},{9,17},{17,25},{... | collective-permute-start | bytes 2359304 | tf_op jit(solution)/shard_map/ppermute | solution.py:257
  91.4 1.3 add_convert_fusion.1.refs_4_
  92.8 2.3 collective-permute-start.16
  95.1 5.7 %collective-permute-done.5.refs_1_ = bf16[2,512,384]{2,1,0:T(8,128)(2,1)S(1)} collective-permute-done((bf16[2,512,384]{2,1,0:T(8,128)(2,1)S(1)}, bf16[2,512,384]{2,1,0:T(8,128)(2,1)S(1)}, u32[]{:S(2)}, u32[]{:S(2)}) %collective-permute-start.5) | collective-permute-done | bytes 786464 | tf_op jit(solution)/shard_map/ppermute | solution.py:257
  100.8 2.9 %fusion.11 = bf16[2,512,384]{2,1,0:T(8,128)(2,1)} fusion(bf16[2,512,384]{2,1,0:T(8,128)(2,1)S(1)} %collective-permute-done.5.refs_1_, bf16[3,2,512,384]{3,2,1,0:T(8,128)(2,1)} %collective-permute-done.6, bf16[4,2,512,384]{3,2,1,0:T(8,128)(2,1)} %get-tuple-element.18, pred[]{:T(512)S(6)} %ge.12), kind=kLoop, calls=%fused_computation.25 | loop fusion | flops 2752512 | bytes 3145729 | tf_op jit(solution)/shard_map/convert_element_type | solution.py:339
  103.7 5.3 %collective-permute-start.7 = (bf16[2,512,384]{2,1,0:T(8,128)(2,1)}, bf16[2,512,384]{2,1,0:T(8,128)(2,1)}, u32[]{:S(2)}, u32[]{:S(2)}) collective-permute-start(bf16[2,512,384]{2,1,0:T(8,128)(2,1)} %fusion.11), channel_id=1, source_target_pairs={{0,8},{8,16},{16,24},{28,20},{20,12},{12,4},{1,9},{9,17},{17,25},{... | collective-permute-start | bytes 2359304 | tf_op jit(solution)/shard_map/ppermute | solution.py:257
  110.2 1.7 fusion.6
  111.9 4.7 %collective-permute-start.18 = (bf16[2,512,384]{2,1,0:T(8,128)(2,1)S(1)}, bf16[2,512,384]{2,1,0:T(8,128)(2,1)S(1)}, u32[]{:S(2)}, u32[]{:S(2)}) collective-permute-start(bf16[2,512,384]{2,1,0:T(8,128)(2,1)S(1)} %fusion.6), channel_id=1, source_target_pairs={{0,8},{8,16},{16,24},{28,20},{20,12},{12,4},{1,9},{9,17},{17,25},{... | collective-permute-start | bytes 2359304 | tf_op jit(solution)/shard_map/ppermute | solution.py:257
  116.7 1.3 collective-permute-done.7.refs_2_
  117.9 2.9 %fusion.10 = bf16[2,512,384]{2,1,0:T(8,128)(2,1)} fusion(bf16[2,512,384]{2,1,0:T(8,128)(2,1)} %collective-permute-done.7.refs_2_, bf16[3,2,512,384]{3,2,1,0:T(8,128)(2,1)} %collective-permute-done.6, bf16[4,2,512,384]{3,2,1,0:T(8,128)(2,1)} %get-tuple-element.18, pred[]{:T(512)S(6)} %ge.13), kind=kLoop, calls=%fused_computation.23 | loop fusion | flops 2752512 | bytes 3145729 | tf_op jit(solution)/shard_map/convert_element_type | solution.py:339
  120.8 5.3 %collective-permute-start.8 = (bf16[2,512,384]{2,1,0:T(8,128)(2,1)}, bf16[2,512,384]{2,1,0:T(8,128)(2,1)}, u32[]{:S(2)}, u32[]{:S(2)}) collective-permute-start(bf16[2,512,384]{2,1,0:T(8,128)(2,1)} %fusion.10), channel_id=1, source_target_pairs={{0,8},{8,16},{16,24},{28,20},{20,12},{12,4},{1,9},{9,17},{17,25},{... | collective-permute-start | bytes 2359304 | tf_op jit(solution)/shard_map/ppermute | solution.py:257
  126.3 2.7 %fusion.5 = bf16[2,512,384]{2,1,0:T(8,128)(2,1)} fusion(bf16[2,512,384]{2,1,0:T(8,128)(2,1)S(1)} %collective-permute-done.18.refs_6_, bf16[3,2,512,384]{3,2,1,0:T(8,128)(2,1)} %collective-permute-done.17, bf16[4,2,512,384]{3,2,1,0:T(8,128)(2,1)S(1)} %copy-done.11, pred[]{:T(512)S(6)} %ge.13), kind=kLoop, calls=%fused_computation.13 | loop fusion | flops 2752512 | bytes 3145729 | tf_op jit(solution)/shard_map/convert_element_type | solution.py:339
  128.9 5.3 %collective-permute-start.19 = (bf16[2,512,384]{2,1,0:T(8,128)(2,1)}, bf16[2,512,384]{2,1,0:T(8,128)(2,1)}, u32[]{:S(2)}, u32[]{:S(2)}) collective-permute-start(bf16[2,512,384]{2,1,0:T(8,128)(2,1)} %fusion.5), channel_id=1, source_target_pairs={{0,8},{8,16},{16,24},{28,20},{20,12},{12,4},{1,9},{9,17},{17,25},{... | collective-permute-start | bytes 2359304 | tf_op jit(solution)/shard_map/ppermute | solution.py:257
  135.0 2.0 fusion.9
  137.0 4.4 %collective-permute-start.9 = (bf16[2,512,384]{2,1,0:T(8,128)(2,1)S(1)}, bf16[2,512,384]{2,1,0:T(8,128)(2,1)S(1)}, u32[]{:S(2)}, u32[]{:S(2)}) collective-permute-start(bf16[2,512,384]{2,1,0:T(8,128)(2,1)S(1)} %fusion.9), channel_id=1, source_target_pairs={{0,8},{8,16},{16,24},{28,20},{20,12},{12,4},{1,9},{9,17},{17,25},{... | collective-permute-start | bytes 2359304 | tf_op jit(solution)/shard_map/ppermute | solution.py:257
  141.4 2.0 collective-permute-done.19.refs_7_
  143.4 2.6 fusion.4
  146.0 4.6 %collective-permute-start.20 = (bf16[2,512,384]{2,1,0:T(8,128)(2,1)}, bf16[2,512,384]{2,1,0:T(8,128)(2,1)S(1)}, u32[]{:S(2)}, u32[]{:S(2)}) collective-permute-start(bf16[2,512,384]{2,1,0:T(8,128)(2,1)} %fusion.4), channel_id=1, source_target_pairs={{0,8},{8,16},{16,24},{28,20},{20,12},{12,4},{1,9},{9,17},{17,25},{... | collective-permute-start | bytes 2359304 | tf_op jit(solution)/shard_map/ppermute | solution.py:257
  151.7 1.3 fusion.2
  153.6 6.8 %collective-permute-done.20 = bf16[2,512,384]{2,1,0:T(8,128)(2,1)S(1)} collective-permute-done((bf16[2,512,384]{2,1,0:T(8,128)(2,1)}, bf16[2,512,384]{2,1,0:T(8,128)(2,1)S(1)}, u32[]{:S(2)}, u32[]{:S(2)}) %collective-permute-start.20) | collective-permute-done | bytes 786464 | tf_op jit(solution)/shard_map/ppermute | solution.py:257
  160.3 1.3 fusion
  162.0 5.2 %collective-permute-start.22 = (bf16[2,512,384]{2,1,0:T(8,128)(2,1)S(1)}, bf16[2,512,384]{2,1,0:T(8,128)(2,1)}, u32[]{:S(2)}, u32[]{:S(2)}) collective-permute-start(bf16[2,512,384]{2,1,0:T(8,128)(2,1)S(1)} %add_convert_fusion.3.refs_0_), channel_id=1, source_target_pairs={{0,8},{8,16},{16,24},{28,20},{20,12},{12,4},{1,9},{9,17},{17,25},{... | collective-permute-start | bytes 2359304 | tf_op jit(solution)/shard_map/ppermute | solution.py:257
  170.7 2.3 collective-permute-start.29
  173.0 2.8 %collective-permute-done.22.refs_1_ = bf16[2,512,384]{2,1,0:T(8,128)(2,1)} collective-permute-done((bf16[2,512,384]{2,1,0:T(8,128)(2,1)S(1)}, bf16[2,512,384]{2,1,0:T(8,128)(2,1)}, u32[]{:S(2)}, u32[]{:S(2)}) %collective-permute-start.22) | collective-permute-done | bytes 786464 | tf_op jit(solution)/shard_map/ppermute | solution.py:257
  175.8 1.9 collective-permute-start.30
  177.7 6.2 %shard_map.79 = bf16[56,32,384]{2,1,0:T(8,128)(2,1)} custom-call(s32[112]{0:T(128)} %pad_add_fusion.1.table_ref, s32[3]{0:T(128)} %pad_add_fusion.meta_ref, bf16[4,224,2048]{2,1,0:T(8,128)(2,1)} %mine_ref.5, bf16[4,224,2048]{2,1,0:T(8,128)(2,1)} %collective-permute-done.23.theirs_ref, bf16[2,512,384]{2,1,0:T(8,128)(2,1)} %copy-done.5, ...), custom_call_target="tpu_custom_call" | custom-call | flops 2818572288 | bytes 8716288 | tf_op jit(solution)/shard_map/pallas_call | solution.py:212
  183.9 1.5 constant_dynamic-slice_fusion.3
  186.3 8.3 %collective-permute-start.24 = (bf16[4,7,4,8,384]{4,3,1,0,2:T(8,128)(2,1)}, bf16[4,7,4,8,384]{4,3,1,0,2:T(8,128)(2,1)}, u32[]{:S(2)}, u32[]{:S(2)}) collective-permute-start(bf16[4,7,4,8,384]{4,3,1,0,2:T(8,128)(2,1)} %bitcast.135), channel_id=1, source_target_pairs={{0,4},{4,0},{8,12},{12,8},{16,20},{20,16},{24,28},{28,24},{1,5},{5... | collective-permute-start | bytes 2064392 | tf_op jit(solution)/shard_map/ppermute | solution.py:272
  194.6 1.6 collective-permute-start.28
  196.1 1.5 collective-permute-start.31
  197.7 1.3 fusion.15
  199.7 2.4 collective-permute-start.27
  203.2 5.9 %shard_map.80.refs_0_ = bf16[56,32,384]{2,1,0:T(8,128)(2,1)} custom-call(s32[112]{0:T(128)} %pad_add_fusion.1.table_ref, s32[3]{0:T(128)} %pad_add_fusion.meta_ref, bf16[4,224,2048]{2,1,0:T(8,128)(2,1)} %mine_ref.5, bf16[4,224,2048]{2,1,0:T(8,128)(2,1)} %collective-permute-done.23.theirs_ref, bf16[2,512,384]{2,1,0:T(8,128)(2,1)} %copy-done.1, ...), custom_call_target="tpu_custom_call" | custom-call | flops 1409286144 | bytes 8716288 | tf_op jit(solution)/shard_map/pallas_call | solution.py:212
  210.4 3.7 %shard_map.81 = bf16[56,32,384]{2,1,0:T(8,128)(2,1)} custom-call(s32[112]{0:T(128)} %pad_add_fusion.1.table_ref, s32[3]{0:T(128)} %pad_add_fusion.meta_ref, bf16[4,224,2048]{2,1,0:T(8,128)(2,1)} %mine_ref.5, bf16[4,224,2048]{2,1,0:T(8,128)(2,1)} %collective-permute-done.23.theirs_ref, bf16[56,32,384]{2,1,0:T(8,128)(2,1)} %shard_map.80.refs_0_, ...), custom_call_target="tpu_custom_call" | custom-call | flops 704643072 | bytes 8716288 | tf_op jit(solution)/shard_map/pallas_call | solution.py:212
  214.1 2.1 dynamic-slice_bitcast_fusion
  216.3 9.1 %collective-permute-start.32 = (bf16[4,7,4,8,384]{4,3,2,1,0:T(8,128)(2,1)}, bf16[4,7,4,8,384]{4,3,2,1,0:T(8,128)(2,1)S(1)}, u32[]{:S(2)}, u32[]{:S(2)}) collective-permute-start(bf16[4,7,4,8,384]{4,3,2,1,0:T(8,128)(2,1)} %dynamic-slice_bitcast_fusion), channel_id=1, source_target_pairs={{0,4},{4,0},{8,12},{12,8},{16,20},{20,16},{24,28},{28,24},{1,5},{5... | collective-permute-start | bytes 2064392 | tf_op jit(solution)/shard_map/ppermute | solution.py:272
  225.5 1.9 collective-permute-done.32
  227.6 1.6 collective-permute-start.35
  229.7 1.5 collective-permute-start.33
  231.3 4.5 %collective-permute-done.35 = bf16[4,7,8,384]{3,2,1,0:T(8,128)(2,1)S(1)} collective-permute-done((bf16[4,7,8,384]{3,2,1,0:T(8,128)(2,1)S(1)}, bf16[4,7,8,384]{3,2,1,0:T(8,128)(2,1)S(1)}, u32[]{:S(2)}, u32[]{:S(2)}) %collective-permute-start.35) | collective-permute-done | bytes 172064 | tf_op jit(solution)/shard_map/ppermute | solution.py:277
  235.9 3.1 %collective-permute-done.34 = bf16[4,7,8,384]{3,2,1,0:T(8,128)(2,1)S(1)} collective-permute-done((bf16[4,7,8,384]{3,2,1,0:T(8,128)(2,1)S(1)}, bf16[4,7,8,384]{3,2,1,0:T(8,128)(2,1)S(1)}, u32[]{:S(2)}, u32[]{:S(2)}) %collective-permute-start.34) | collective-permute-done | bytes 172064 | tf_op jit(solution)/shard_map/ppermute | solution.py:277
  239.2 3.4 %collective-permute-start.38 = (bf16[7,8,768]{2,1,0:T(8,128)(2,1)S(1)}, bf16[7,8,768]{2,1,0:T(8,128)(2,1)S(1)}, u32[]{:S(2)}, u32[]{:S(2)}) collective-permute-start(bf16[7,8,768]{2,1,0:T(8,128)(2,1)S(1)} %get-tuple-element.42), channel_id=1, source_target_pairs={{0,24},{4,28},{8,0},{12,4},{16,8},{20,12},{24,16},{28,20},{1,25},{... | collective-permute-start | bytes 258056 | tf_op jit(solution)/shard_map/ppermute | solution.py:283
  242.8 1.9 collective-permute-start.36
  245.6 5.6 %collective-permute-done.37 = bf16[7,8,768]{2,1,0:T(8,128)(2,1)S(1)} collective-permute-done((bf16[7,8,768]{2,1,0:T(8,128)(2,1)S(1)}, bf16[7,8,768]{2,1,0:T(8,128)(2,1)S(1)}, u32[]{:S(2)}, u32[]{:S(2)}) %collective-permute-start.37) | collective-permute-done | bytes 86048 | tf_op jit(solution)/shard_map/ppermute | solution.py:283
  251.8 1.3 maximum_maximum_fusion
  253.1 1.6 collective-permute-start.40
  254.7 1.4 collective-permute-start.41
  256.1 2.5 collective-permute-done.40
  258.5 1.5 collective-permute-done.41
  (113 shorter events, 19.3 us)
Async XLA Ops:
  14.9 14.8 %collective-permute-start = (bf16[3,2,512,384]{3,2,1,0:T(8,128)(2,1)}, bf16[3,2,512,384]{3,2,1,0:T(8,128)(2,1)S(1)}, u32[]{:S(2)}, u32[]{:S(2)}) collective-permute-start(bf16[3,2,512,384]{3,2,1,0:T(8,128)(2,1)} %get-tuple-element.17), channel_id=1, source_target_pairs={{0,4},{4,0},{8,12},{12,8},{16,20},{20,16},{24,28},{28,24},{1,5},{5... | collective-permute-start | bytes 7077896 | tf_op jit(solution)/shard_map/ppermute | solution.py:264
  15.4 14.2 %copy-start.10 = (bf16[4,2,512,384]{3,2,1,0:T(8,128)(2,1)S(1)}, bf16[4,2,512,384]{3,2,1,0:T(8,128)(2,1)}, u32[]{:S(2)}) copy-start(bf16[4,2,512,384]{3,2,1,0:T(8,128)(2,1)} %get-tuple-element.16) | copy-start | bytes 9437188
  29.6 5.3 %collective-permute-start.11 = (bf16[3,2,512,384]{3,2,1,0:T(8,128)(2,1)}, bf16[3,2,512,384]{3,2,1,0:T(8,128)(2,1)S(1)}, u32[]{:S(2)}, u32[]{:S(2)}) collective-permute-start(bf16[3,2,512,384]{3,2,1,0:T(8,128)(2,1)} %get-tuple-element.22), channel_id=1, source_target_pairs={{0,4},{4,0},{8,12},{12,8},{16,20},{20,16},{24,28},{28,24},{1,5},{5... | collective-permute-start | bytes 7077896 | tf_op jit(solution)/shard_map/ppermute | solution.py:264
  29.9 14.4 %collective-permute-start.1 = (bf16[2,512,384]{2,1,0:T(8,128)(2,1)S(1)}, bf16[2,512,384]{2,1,0:T(8,128)(2,1)S(1)}, u32[]{:S(2)}, u32[]{:S(2)}) collective-permute-start(bf16[2,512,384]{2,1,0:T(8,128)(2,1)S(1)} %fusion.16), channel_id=1, source_target_pairs={{0,8},{28,20},{1,9},{29,21},{2,10},{30,22},{3,11},{31,23}} | collective-permute-start | bytes 2359304 | tf_op jit(solution)/shard_map/ppermute | solution.py:257
  36.2 16.5 %copy-start.9 = (bf16[4,2,512,384]{3,2,1,0:T(8,128)(2,1)S(1)}, bf16[4,2,512,384]{3,2,1,0:T(8,128)(2,1)}, u32[]{:S(2)}) copy-start(bf16[4,2,512,384]{3,2,1,0:T(8,128)(2,1)} %get-tuple-element.21) | copy-start | bytes 9437188
  36.2 16.5 %collective-permute-start.12 = (bf16[2,512,384]{2,1,0:T(8,128)(2,1)S(1)}, bf16[2,512,384]{2,1,0:T(8,128)(2,1)S(1)}, u32[]{:S(2)}, u32[]{:S(2)}) collective-permute-start(bf16[2,512,384]{2,1,0:T(8,128)(2,1)S(1)} %fusion.17), channel_id=1, source_target_pairs={{0,8},{28,20},{1,9},{29,21},{2,10},{30,22},{3,11},{31,23}} | collective-permute-start | bytes 2359304 | tf_op jit(solution)/shard_map/ppermute | solution.py:257
  44.6 16.5 %collective-permute-start.2 = (bf16[2,512,384]{2,1,0:T(8,128)(2,1)S(1)}, bf16[2,512,384]{2,1,0:T(8,128)(2,1)S(1)}, u32[]{:S(2)}, u32[]{:S(2)}) collective-permute-start(bf16[2,512,384]{2,1,0:T(8,128)(2,1)S(1)} %fusion.12), channel_id=1, source_target_pairs={{0,8},{8,16},{28,20},{20,12},{1,9},{9,17},{29,21},{21,13},{2,10},{... | collective-permute-start | bytes 2359304 | tf_op jit(solution)/shard_map/ppermute | solution.py:257
  53.1 16.5 %collective-permute-start.13 = (bf16[2,512,384]{2,1,0:T(8,128)(2,1)S(1)}, bf16[2,512,384]{2,1,0:T(8,128)(2,1)S(1)}, u32[]{:S(2)}, u32[]{:S(2)}) collective-permute-start(bf16[2,512,384]{2,1,0:T(8,128)(2,1)S(1)} %fusion.7), channel_id=1, source_target_pairs={{0,8},{8,16},{28,20},{20,12},{1,9},{9,17},{29,21},{21,13},{2,10},{... | collective-permute-start | bytes 2359304 | tf_op jit(solution)/shard_map/ppermute | solution.py:257
  61.5 16.5 %collective-permute-start.3 = (bf16[2,512,384]{2,1,0:T(8,128)(2,1)S(1)}, bf16[2,512,384]{2,1,0:T(8,128)(2,1)S(1)}, u32[]{:S(2)}, u32[]{:S(2)}) collective-permute-start(bf16[2,512,384]{2,1,0:T(8,128)(2,1)S(1)} %fusion.13), channel_id=1, source_target_pairs={{0,8},{8,16},{16,24},{28,20},{20,12},{12,4},{1,9},{9,17},{17,25},{... | collective-permute-start | bytes 2359304 | tf_op jit(solution)/shard_map/ppermute | solution.py:257
  65.9 29.2 %collective-permute-start.6 = (bf16[3,2,512,384]{3,2,1,0:T(8,128)(2,1)}, bf16[3,2,512,384]{3,2,1,0:T(8,128)(2,1)}, u32[]{:S(2)}, u32[]{:S(2)}) collective-permute-start(bf16[3,2,512,384]{3,2,1,0:T(8,128)(2,1)} %get-tuple-element.19), channel_id=1, source_target_pairs={{0,4},{4,0},{8,12},{12,8},{16,20},{20,16},{24,28},{28,24},{1,5},{5... | collective-permute-start | bytes 7077896 | tf_op jit(solution)/shard_map/ppermute | solution.py:264
  69.9 16.5 %collective-permute-start.14 = (bf16[2,512,384]{2,1,0:T(8,128)(2,1)S(1)}, bf16[2,512,384]{2,1,0:T(8,128)(2,1)S(1)}, u32[]{:S(2)}, u32[]{:S(2)}) collective-permute-start(bf16[2,512,384]{2,1,0:T(8,128)(2,1)S(1)} %fusion.8), channel_id=1, source_target_pairs={{0,8},{8,16},{16,24},{28,20},{20,12},{12,4},{1,9},{9,17},{17,25},{... | collective-permute-start | bytes 2359304 | tf_op jit(solution)/shard_map/ppermute | solution.py:257
  78.2 8.5 %collective-permute-start.4 = (bf16[2,512,384]{2,1,0:T(8,128)(2,1)S(1)}, bf16[2,512,384]{2,1,0:T(8,128)(2,1)S(1)}, u32[]{:S(2)}, u32[]{:S(2)}) collective-permute-start(bf16[2,512,384]{2,1,0:T(8,128)(2,1)S(1)} %fusion.3), channel_id=1, source_target_pairs={{0,4},{4,0},{8,12},{12,8},{16,20},{20,16},{24,28},{28,24},{1,5},{5... | collective-permute-start | bytes 2359304 | tf_op jit(solution)/shard_map/ppermute | solution.py:329
  78.3 30.7 %collective-permute-start.17 = (bf16[3,2,512,384]{3,2,1,0:T(8,128)(2,1)}, bf16[3,2,512,384]{3,2,1,0:T(8,128)(2,1)}, u32[]{:S(2)}, u32[]{:S(2)}) collective-permute-start(bf16[3,2,512,384]{3,2,1,0:T(8,128)(2,1)} %get-tuple-element.24), channel_id=1, source_target_pairs={{0,4},{4,0},{8,12},{12,8},{16,20},{20,16},{24,28},{28,24},{1,5},{5... | collective-permute-start | bytes 7077896 | tf_op jit(solution)/shard_map/ppermute | solution.py:264
  86.6 4.8 %collective-permute-start.15 = (bf16[2,512,384]{2,1,0:T(8,128)(2,1)S(1)}, bf16[2,512,384]{2,1,0:T(8,128)(2,1)}, u32[]{:S(2)}, u32[]{:S(2)}) collective-permute-start(bf16[2,512,384]{2,1,0:T(8,128)(2,1)S(1)} %fusion.1), channel_id=1, source_target_pairs={{0,4},{4,0},{8,12},{12,8},{16,20},{20,16},{24,28},{28,24},{1,5},{5... | collective-permute-start | bytes 2359304 | tf_op jit(solution)/shard_map/ppermute | solution.py:329
  86.9 16.8 %copy-start.5 = (bf16[2,512,384]{2,1,0:T(8,128)(2,1)}, bf16[2,512,384]{2,1,0:T(8,128)(2,1)S(1)}, u32[]{:S(2)}) copy-start(bf16[2,512,384]{2,1,0:T(8,128)(2,1)S(1)} %add_convert_fusion.4.refs_0_) | copy-start | bytes 2359300
  87.0 13.9 %collective-permute-start.5 = (bf16[2,512,384]{2,1,0:T(8,128)(2,1)S(1)}, bf16[2,512,384]{2,1,0:T(8,128)(2,1)S(1)}, u32[]{:S(2)}, u32[]{:S(2)}) collective-permute-start(bf16[2,512,384]{2,1,0:T(8,128)(2,1)S(1)} %add_convert_fusion.4.refs_0_), channel_id=1, source_target_pairs={{0,8},{8,16},{16,24},{28,20},{20,12},{12,4},{1,9},{9,17},{17,25},{... | collective-permute-start | bytes 2359304 | tf_op jit(solution)/shard_map/ppermute | solution.py:257
  92.7 11.0 %copy-start.7 = (bf16[2,512,384]{2,1,0:T(8,128)(2,1)}, bf16[2,512,384]{2,1,0:T(8,128)(2,1)S(1)}, u32[]{:S(2)}) copy-start(bf16[2,512,384]{2,1,0:T(8,128)(2,1)S(1)} %add_convert_fusion.1.refs_4_) | copy-start | bytes 2359300
  92.8 16.5 %collective-permute-start.16 = (bf16[2,512,384]{2,1,0:T(8,128)(2,1)S(1)}, bf16[2,512,384]{2,1,0:T(8,128)(2,1)S(1)}, u32[]{:S(2)}, u32[]{:S(2)}) collective-permute-start(bf16[2,512,384]{2,1,0:T(8,128)(2,1)S(1)} %add_convert_fusion.1.refs_4_), channel_id=1, source_target_pairs={{0,8},{8,16},{16,24},{28,20},{20,12},{12,4},{1,9},{9,17},{17,25},{... | collective-permute-start | bytes 2359304 | tf_op jit(solution)/shard_map/ppermute | solution.py:257
  100.8 2.9 %copy-start.12 = (bf16[2,512,384]{2,1,0:T(8,128)(2,1)}, bf16[2,512,384]{2,1,0:T(8,128)(2,1)S(1)}, u32[]{:S(2)}) copy-start(bf16[2,512,384]{2,1,0:T(8,128)(2,1)S(1)} %collective-permute-done.5.refs_1_) | copy-start | bytes 2359300
  103.7 14.2 %collective-permute-start.7 = (bf16[2,512,384]{2,1,0:T(8,128)(2,1)}, bf16[2,512,384]{2,1,0:T(8,128)(2,1)}, u32[]{:S(2)}, u32[]{:S(2)}) collective-permute-start(bf16[2,512,384]{2,1,0:T(8,128)(2,1)} %fusion.11), channel_id=1, source_target_pairs={{0,8},{8,16},{16,24},{28,20},{20,12},{12,4},{1,9},{9,17},{17,25},{... | collective-permute-start | bytes 2359304 | tf_op jit(solution)/shard_map/ppermute | solution.py:257
  109.3 0.9 copy-start.13
  111.9 14.4 %copy-start.11 = (bf16[4,2,512,384]{3,2,1,0:T(8,128)(2,1)S(1)}, bf16[4,2,512,384]{3,2,1,0:T(8,128)(2,1)}, u32[]{:S(2)}) copy-start(bf16[4,2,512,384]{3,2,1,0:T(8,128)(2,1)} %get-tuple-element.23) | copy-start | bytes 9437188
  111.9 14.4 %collective-permute-start.18 = (bf16[2,512,384]{2,1,0:T(8,128)(2,1)S(1)}, bf16[2,512,384]{2,1,0:T(8,128)(2,1)S(1)}, u32[]{:S(2)}, u32[]{:S(2)}) collective-permute-start(bf16[2,512,384]{2,1,0:T(8,128)(2,1)S(1)} %fusion.6), channel_id=1, source_target_pairs={{0,8},{8,16},{16,24},{28,20},{20,12},{12,4},{1,9},{9,17},{17,25},{... | collective-permute-start | bytes 2359304 | tf_op jit(solution)/shard_map/ppermute | solution.py:257
  116.6 52.4 %collective-permute-start.23 = (bf16[4,224,2048]{2,1,0:T(8,128)(2,1)}, bf16[4,224,2048]{2,1,0:T(8,128)(2,1)}, u32[]{:S(2)}, u32[]{:S(2)}) collective-permute-start(bf16[4,224,2048]{2,1,0:T(8,128)(2,1)} %mine_ref.5), channel_id=1, source_target_pairs={{0,4},{4,0},{8,12},{12,8},{16,20},{20,16},{24,28},{28,24},{1,5},{5... | collective-permute-start | bytes 11010056 | tf_op jit(solution)/shard_map/ppermute | solution.py:322
  120.8 14.2 %collective-permute-start.8 = (bf16[2,512,384]{2,1,0:T(8,128)(2,1)}, bf16[2,512,384]{2,1,0:T(8,128)(2,1)}, u32[]{:S(2)}, u32[]{:S(2)}) collective-permute-start(bf16[2,512,384]{2,1,0:T(8,128)(2,1)} %fusion.10), channel_id=1, source_target_pairs={{0,8},{8,16},{16,24},{28,20},{20,12},{12,4},{1,9},{9,17},{17,25},{... | collective-permute-start | bytes 2359304 | tf_op jit(solution)/shard_map/ppermute | solution.py:257
  126.3 2.7 %copy-start.14 = (bf16[2,512,384]{2,1,0:T(8,128)(2,1)}, bf16[2,512,384]{2,1,0:T(8,128)(2,1)S(1)}, u32[]{:S(2)}) copy-start(bf16[2,512,384]{2,1,0:T(8,128)(2,1)S(1)} %collective-permute-done.18.refs_6_) | copy-start | bytes 2359300
  128.9 14.5 %collective-permute-start.19 = (bf16[2,512,384]{2,1,0:T(8,128)(2,1)}, bf16[2,512,384]{2,1,0:T(8,128)(2,1)}, u32[]{:S(2)}, u32[]{:S(2)}) collective-permute-start(bf16[2,512,384]{2,1,0:T(8,128)(2,1)} %fusion.5), channel_id=1, source_target_pairs={{0,8},{8,16},{16,24},{28,20},{20,12},{12,4},{1,9},{9,17},{17,25},{... | collective-permute-start | bytes 2359304 | tf_op jit(solution)/shard_map/ppermute | solution.py:257
  137.0 14.8 %collective-permute-start.9 = (bf16[2,512,384]{2,1,0:T(8,128)(2,1)S(1)}, bf16[2,512,384]{2,1,0:T(8,128)(2,1)S(1)}, u32[]{:S(2)}, u32[]{:S(2)}) collective-permute-start(bf16[2,512,384]{2,1,0:T(8,128)(2,1)S(1)} %fusion.9), channel_id=1, source_target_pairs={{0,8},{8,16},{16,24},{28,20},{20,12},{12,4},{1,9},{9,17},{17,25},{... | collective-permute-start | bytes 2359304 | tf_op jit(solution)/shard_map/ppermute | solution.py:257
  146.0 7.2 %copy-start.16 = (s32[56,4]{0,1:T(4,128)S(1)}, s32[56,4]{0,1:T(4,128)}, u32[]{:S(2)}) copy-start(s32[56,4]{0,1:T(4,128)} %param.11) | copy-start | bytes 2692
  146.0 7.2 %copy-start.17 = (s32[56,4,1]{0,2,1:T(1,128)S(1)}, s32[56,4,1]{0,2,1:T(1,128)}, u32[]{:S(2)}) copy-start(s32[56,4,1]{0,2,1:T(1,128)} %param.10) | copy-start | bytes 2692
  146.0 14.3 %collective-permute-start.20 = (bf16[2,512,384]{2,1,0:T(8,128)(2,1)}, bf16[2,512,384]{2,1,0:T(8,128)(2,1)S(1)}, u32[]{:S(2)}, u32[]{:S(2)}) collective-permute-start(bf16[2,512,384]{2,1,0:T(8,128)(2,1)} %fusion.4), channel_id=1, source_target_pairs={{0,8},{8,16},{16,24},{28,20},{20,12},{12,4},{1,9},{9,17},{17,25},{... | collective-permute-start | bytes 2359304 | tf_op jit(solution)/shard_map/ppermute | solution.py:257
  153.1 8.7 %collective-permute-start.10 = (bf16[2,512,384]{2,1,0:T(8,128)(2,1)S(1)}, bf16[2,512,384]{2,1,0:T(8,128)(2,1)S(1)}, u32[]{:S(2)}, u32[]{:S(2)}) collective-permute-start(bf16[2,512,384]{2,1,0:T(8,128)(2,1)S(1)} %fusion.2), channel_id=1, source_target_pairs={{0,4},{4,0},{8,12},{12,8},{16,20},{20,16},{24,28},{28,24},{1,5},{5... | collective-permute-start | bytes 2359304 | tf_op jit(solution)/shard_map/ppermute | solution.py:329
  161.7 8.8 %collective-permute-start.21 = (bf16[2,512,384]{2,1,0:T(8,128)(2,1)S(1)}, bf16[2,512,384]{2,1,0:T(8,128)(2,1)S(1)}, u32[]{:S(2)}, u32[]{:S(2)}) collective-permute-start(bf16[2,512,384]{2,1,0:T(8,128)(2,1)S(1)} %fusion), channel_id=1, source_target_pairs={{0,4},{4,0},{8,12},{12,8},{16,20},{20,16},{24,28},{28,24},{1,5},{5... | collective-permute-start | bytes 2359304 | tf_op jit(solution)/shard_map/ppermute | solution.py:329
  162.0 8.3 %copy-start.1 = (bf16[2,512,384]{2,1,0:T(8,128)(2,1)}, bf16[2,512,384]{2,1,0:T(8,128)(2,1)S(1)}, u32[]{:S(2)}) copy-start(bf16[2,512,384]{2,1,0:T(8,128)(2,1)S(1)} %add_convert_fusion.3.refs_0_) | copy-start | bytes 2359300
  162.0 13.8 %collective-permute-start.22 = (bf16[2,512,384]{2,1,0:T(8,128)(2,1)S(1)}, bf16[2,512,384]{2,1,0:T(8,128)(2,1)}, u32[]{:S(2)}, u32[]{:S(2)}) collective-permute-start(bf16[2,512,384]{2,1,0:T(8,128)(2,1)S(1)} %add_convert_fusion.3.refs_0_), channel_id=1, source_target_pairs={{0,8},{8,16},{16,24},{28,20},{20,12},{12,4},{1,9},{9,17},{17,25},{... | collective-permute-start | bytes 2359304 | tf_op jit(solution)/shard_map/ppermute | solution.py:257
  170.7 13.2 %copy-start.3 = (bf16[2,512,384]{2,1,0:T(8,128)(2,1)}, bf16[2,512,384]{2,1,0:T(8,128)(2,1)S(1)}, u32[]{:S(2)}) copy-start(bf16[2,512,384]{2,1,0:T(8,128)(2,1)S(1)} %add_convert_fusion.refs_2_) | copy-start | bytes 2359300
  170.7 25.5 %collective-permute-start.29 = (bf16[2,512,384]{2,1,0:T(8,128)(2,1)S(1)}, bf16[2,512,384]{2,1,0:T(8,128)(2,1)}, u32[]{:S(2)}, u32[]{:S(2)}) collective-permute-start(bf16[2,512,384]{2,1,0:T(8,128)(2,1)S(1)} %add_convert_fusion.refs_2_), channel_id=1, source_target_pairs={{0,8},{8,16},{16,24},{28,20},{20,12},{12,4},{1,9},{9,17},{17,25},{... | collective-permute-start | bytes 2359304 | tf_op jit(solution)/shard_map/ppermute | solution.py:257
  175.8 34.6 %collective-permute-start.30 = (bf16[4,448,512]{2,1,0:T(8,128)(2,1)S(1)}, bf16[4,448,512]{2,1,0:T(8,128)(2,1)}, u32[]{:S(2)}, u32[]{:S(2)}) collective-permute-start(bf16[4,448,512]{2,1,0:T(8,128)(2,1)S(1)} %pad_maximum_fusion), channel_id=1, source_target_pairs={{24,16},{4,12},{25,17},{5,13},{26,18},{6,14},{27,19},{7,15}} | collective-permute-start | bytes 5505032 | tf_op jit(solution)/shard_map/ppermute | solution.py:356
  186.3 11.4 %collective-permute-start.24 = (bf16[4,7,4,8,384]{4,3,1,0,2:T(8,128)(2,1)}, bf16[4,7,4,8,384]{4,3,1,0,2:T(8,128)(2,1)}, u32[]{:S(2)}, u32[]{:S(2)}) collective-permute-start(bf16[4,7,4,8,384]{4,3,1,0,2:T(8,128)(2,1)} %bitcast.135), channel_id=1, source_target_pairs={{0,4},{4,0},{8,12},{12,8},{16,20},{20,16},{24,28},{28,24},{1,5},{5... | collective-permute-start | bytes 2064392 | tf_op jit(solution)/shard_map/ppermute | solution.py:272
  194.6 8.1 %collective-permute-start.28 = (bf16[2,512,384]{2,1,0:T(8,128)(2,1)}, bf16[2,512,384]{2,1,0:T(8,128)(2,1)}, u32[]{:S(2)}, u32[]{:S(2)}) collective-permute-start(bf16[2,512,384]{2,1,0:T(8,128)(2,1)} %collective-permute-done.22.refs_1_), channel_id=1, source_target_pairs={{8,16},{16,24},{20,12},{12,4},{9,17},{17,25},{21,13},{13,5},{10,18... | collective-permute-start | bytes 2359304 | tf_op jit(solution)/shard_map/ppermute | solution.py:257
  196.1 14.3 %collective-permute-start.31 = (bf16[2,512,384]{2,1,0:T(8,128)(2,1)}, bf16[2,512,384]{2,1,0:T(8,128)(2,1)}, u32[]{:S(2)}, u32[]{:S(2)}) collective-permute-start(bf16[2,512,384]{2,1,0:T(8,128)(2,1)} %collective-permute-done.29.refs_3_), channel_id=1, source_target_pairs={{8,16},{16,24},{20,12},{12,4},{9,17},{17,25},{21,13},{13,5},{10,18... | collective-permute-start | bytes 2359304 | tf_op jit(solution)/shard_map/ppermute | solution.py:257
  199.7 9.4 %collective-permute-start.27 = (bf16[4,7,8,384]{3,2,1,0:T(8,128)(2,1)}, bf16[4,7,8,384]{3,2,1,0:T(8,128)(2,1)S(1)}, u32[]{:S(2)}, u32[]{:S(2)}) collective-permute-start(bf16[4,7,8,384]{3,2,1,0:T(8,128)(2,1)} %get-tuple-element.38), channel_id=1, source_target_pairs={{0,3},{1,2},{2,1},{3,0},{4,7},{5,6},{6,5},{7,4},{8,11},{9,10},{10,... | collective-permute-start | bytes 516104 | tf_op jit(solution)/shard_map/ppermute | solution.py:277
  202.1 8.1 %collective-permute-start.26 = (bf16[4,7,8,384]{3,2,1,0:T(8,128)(2,1)S(1)}, bf16[4,7,8,384]{3,2,1,0:T(8,128)(2,1)S(1)}, u32[]{:S(2)}, u32[]{:S(2)}) collective-permute-start(bf16[4,7,8,384]{3,2,1,0:T(8,128)(2,1)S(1)} %get-tuple-element.39), channel_id=1, source_target_pairs={{0,2},{1,3},{2,0},{3,1},{4,6},{5,7},{6,4},{7,5},{8,10},{9,11},{10,... | collective-permute-start | bytes 516104 | tf_op jit(solution)/shard_map/ppermute | solution.py:277
  202.7 7.6 %collective-permute-start.25 = (bf16[4,7,8,384]{3,2,1,0:T(8,128)(2,1)S(1)}, bf16[4,7,8,384]{3,2,1,0:T(8,128)(2,1)S(1)}, u32[]{:S(2)}, u32[]{:S(2)}) collective-permute-start(bf16[4,7,8,384]{3,2,1,0:T(8,128)(2,1)S(1)} %get-tuple-element.37), channel_id=1, source_target_pairs={{0,1},{1,0},{2,3},{3,2},{4,5},{5,4},{6,7},{7,6},{8,9},{9,8},{10,11... | collective-permute-start | bytes 516104 | tf_op jit(solution)/shard_map/ppermute | solution.py:277
  210.4 15.0 %copy-start.8 = (bf16[2,512,384]{2,1,0:T(8,128)(2,1)S(1)}, bf16[2,512,384]{2,1,0:T(8,128)(2,1)}, u32[]{:S(2)}) copy-start(bf16[2,512,384]{2,1,0:T(8,128)(2,1)} %copy-done.7) | copy-start | bytes 2359300
  214.1 13.2 %copy-start = (bf16[56,32,384]{2,1,0:T(8,128)(2,1)S(1)}, bf16[56,32,384]{2,1,0:T(8,128)(2,1)}, u32[]{:S(2)}) copy-start(bf16[56,32,384]{2,1,0:T(8,128)(2,1)} %shard_map.81) | copy-start | bytes 4128772
  216.3 11.1 %collective-permute-start.32 = (bf16[4,7,4,8,384]{4,3,2,1,0:T(8,128)(2,1)}, bf16[4,7,4,8,384]{4,3,2,1,0:T(8,128)(2,1)S(1)}, u32[]{:S(2)}, u32[]{:S(2)}) collective-permute-start(bf16[4,7,4,8,384]{4,3,2,1,0:T(8,128)(2,1)} %dynamic-slice_bitcast_fusion), channel_id=1, source_target_pairs={{0,4},{4,0},{8,12},{12,8},{16,20},{20,16},{24,28},{28,24},{1,5},{5... | collective-permute-start | bytes 2064392 | tf_op jit(solution)/shard_map/ppermute | solution.py:272
  225.4 5.8 %copy-start.6 = (bf16[2,512,384]{2,1,0:T(8,128)(2,1)S(1)}, bf16[2,512,384]{2,1,0:T(8,128)(2,1)}, u32[]{:S(2)}) copy-start(bf16[2,512,384]{2,1,0:T(8,128)(2,1)} %copy-done.5) | copy-start | bytes 2359300
  225.5 5.8 %copy-start.4 = (bf16[2,512,384]{2,1,0:T(8,128)(2,1)S(1)}, bf16[2,512,384]{2,1,0:T(8,128)(2,1)}, u32[]{:S(2)}) copy-start(bf16[2,512,384]{2,1,0:T(8,128)(2,1)} %copy-done.3) | copy-start | bytes 2359300
  227.6 17.1 %copy-start.2 = (bf16[2,512,384]{2,1,0:T(8,128)(2,1)S(1)}, bf16[2,512,384]{2,1,0:T(8,128)(2,1)}, u32[]{:S(2)}) copy-start(bf16[2,512,384]{2,1,0:T(8,128)(2,1)} %copy-done.1) | copy-start | bytes 2359300
  227.6 8.2 %collective-permute-start.35 = (bf16[4,7,8,384]{3,2,1,0:T(8,128)(2,1)S(1)}, bf16[4,7,8,384]{3,2,1,0:T(8,128)(2,1)S(1)}, u32[]{:S(2)}, u32[]{:S(2)}) collective-permute-start(bf16[4,7,8,384]{3,2,1,0:T(8,128)(2,1)S(1)} %get-tuple-element.35), channel_id=1, source_target_pairs={{0,3},{1,2},{2,1},{3,0},{4,7},{5,6},{6,5},{7,4},{8,11},{9,10},{10,... | collective-permute-start | bytes 516104 | tf_op jit(solution)/shard_map/ppermute | solution.py:277
  229.2 9.7 %collective-permute-start.34 = (bf16[4,7,8,384]{3,2,1,0:T(8,128)(2,1)S(1)}, bf16[4,7,8,384]{3,2,1,0:T(8,128)(2,1)S(1)}, u32[]{:S(2)}, u32[]{:S(2)}) collective-permute-start(bf16[4,7,8,384]{3,2,1,0:T(8,128)(2,1)S(1)} %get-tuple-element.36), channel_id=1, source_target_pairs={{0,2},{1,3},{2,0},{3,1},{4,6},{5,7},{6,4},{7,5},{8,10},{9,11},{10,... | collective-permute-start | bytes 516104 | tf_op jit(solution)/shard_map/ppermute | solution.py:277
  229.7 9.3 %collective-permute-start.33 = (bf16[4,7,8,384]{3,2,1,0:T(8,128)(2,1)S(1)}, bf16[4,7,8,384]{3,2,1,0:T(8,128)(2,1)S(1)}, u32[]{:S(2)}, u32[]{:S(2)}) collective-permute-start(bf16[4,7,8,384]{3,2,1,0:T(8,128)(2,1)S(1)} %get-tuple-element.34), channel_id=1, source_target_pairs={{0,1},{1,0},{2,3},{3,2},{4,5},{5,4},{6,7},{7,6},{8,9},{9,8},{10,11... | collective-permute-start | bytes 516104 | tf_op jit(solution)/shard_map/ppermute | solution.py:277
  239.2 6.4 %collective-permute-start.38 = (bf16[7,8,768]{2,1,0:T(8,128)(2,1)S(1)}, bf16[7,8,768]{2,1,0:T(8,128)(2,1)S(1)}, u32[]{:S(2)}, u32[]{:S(2)}) collective-permute-start(bf16[7,8,768]{2,1,0:T(8,128)(2,1)S(1)} %get-tuple-element.42), channel_id=1, source_target_pairs={{0,24},{4,28},{8,0},{12,4},{16,8},{20,12},{24,16},{28,20},{1,25},{... | collective-permute-start | bytes 258056 | tf_op jit(solution)/shard_map/ppermute | solution.py:283
  242.6 8.5 %collective-permute-start.37 = (bf16[7,8,768]{2,1,0:T(8,128)(2,1)S(1)}, bf16[7,8,768]{2,1,0:T(8,128)(2,1)S(1)}, u32[]{:S(2)}, u32[]{:S(2)}) collective-permute-start(bf16[7,8,768]{2,1,0:T(8,128)(2,1)S(1)} %get-tuple-element.41), channel_id=1, source_target_pairs={{0,16},{4,20},{8,24},{12,28},{16,0},{20,4},{24,8},{28,12},{1,17},{... | collective-permute-start | bytes 258056 | tf_op jit(solution)/shard_map/ppermute | solution.py:283
  242.8 8.3 %collective-permute-start.36 = (bf16[7,8,768]{2,1,0:T(8,128)(2,1)S(1)}, bf16[7,8,768]{2,1,0:T(8,128)(2,1)S(1)}, u32[]{:S(2)}, u32[]{:S(2)}) collective-permute-start(bf16[7,8,768]{2,1,0:T(8,128)(2,1)S(1)} %get-tuple-element.40), channel_id=1, source_target_pairs={{0,8},{4,12},{8,16},{12,20},{16,24},{20,28},{24,0},{28,4},{1,9},{5... | collective-permute-start | bytes 258056 | tf_op jit(solution)/shard_map/ppermute | solution.py:283
  251.2 8.9 %copy-start.15 = (f32[224,768]{1,0:T(8,128)S(1)}, f32[224,768]{1,0:T(8,128)}, u32[]{:S(2)}) copy-start(f32[224,768]{1,0:T(8,128)} %param.9) | copy-start | bytes 2064388
  251.2 4.8 %collective-permute-start.39 = (bf16[7,8,768]{2,1,0:T(8,128)(2,1)S(1)}, bf16[7,8,768]{2,1,0:T(8,128)(2,1)S(1)}, u32[]{:S(2)}, u32[]{:S(2)}) collective-permute-start(bf16[7,8,768]{2,1,0:T(8,128)(2,1)S(1)} %get-tuple-element.31), channel_id=1, source_target_pairs={{0,1},{1,0},{2,3},{3,2},{4,5},{5,4},{6,7},{7,6},{8,9},{9,8},{10,11... | collective-permute-start | bytes 258056 | tf_op jit(solution)/shard_map/ppermute | solution.py:290
  253.1 5.4 %collective-permute-start.40 = (bf16[7,8,768]{2,1,0:T(8,128)(2,1)S(1)}, bf16[7,8,768]{2,1,0:T(8,128)(2,1)S(1)}, u32[]{:S(2)}, u32[]{:S(2)}) collective-permute-start(bf16[7,8,768]{2,1,0:T(8,128)(2,1)S(1)} %get-tuple-element.31), channel_id=1, source_target_pairs={{0,2},{1,3},{2,0},{3,1},{4,6},{5,7},{6,4},{7,5},{8,10},{9,11},{10,... | collective-permute-start | bytes 258056 | tf_op jit(solution)/shard_map/ppermute | solution.py:290
  254.7 5.4 %collective-permute-start.41 = (bf16[7,8,768]{2,1,0:T(8,128)(2,1)S(1)}, bf16[7,8,768]{2,1,0:T(8,128)(2,1)S(1)}, u32[]{:S(2)}, u32[]{:S(2)}) collective-permute-start(bf16[7,8,768]{2,1,0:T(8,128)(2,1)S(1)} %get-tuple-element.31), channel_id=1, source_target_pairs={{0,3},{1,2},{2,1},{3,0},{4,7},{5,6},{6,5},{7,4},{8,11},{9,10},{10,... | collective-permute-start | bytes 258056 | tf_op jit(solution)/shard_map/ppermute | solution.py:290
where the time goes:
time: 262 us; the launch traced here: 261 us
  starting transfers between devices  111 us (42%)
  waiting for transfers between devices  67.9 us (26%)
  Pallas kernels  43.5 us (17%)
  other arithmetic  27.9 us (11%)
  local copies, waits for them, and re-layouts  9.25 us (4%)
    ppermute x18, starting transfers between devices, hop(): return lax.ppermute(value, 'row', up + down)  74.1 us
    ppermute x18, waiting for transfers between devices, hop(): return lax.ppermute(value, 'row', up + down)  46.7 us
    pallas_call x2, Pallas kernels, apply_product(): pl.pallas_call(functools.partial(product_kernel, first), in_specs=[pl.Blo...  27.7 us
    ppermute x2, starting transfers between devices, share_cores(): lax.ppermute(pick(total, 1 - core, 1), 'row', pair)  17.4 us
    pallas_call x3, Pallas kernels, apply_update(): pl.pallas_call(functools.partial(update_kernel, places, has_base), out_sh...  15.8 us
    convert_element_type x6, other arithmetic, per_device(): (send.astype(F32) + jnp.where(upstream >= t - 1, 0.0, late)).astype(BF16)  14.7 us
    convert_element_type x18, other arithmetic, add16(): functools.reduce(lambda a, b: a + b, [t.astype(F32) for t in terms])  9.47 us
    ppermute x6, waiting for transfers between devices, share_col(): lax.ppermute(pick(total, col ^ d, 2), 'col', turns[d - 1])  8.88 us
  transfers between devices with their start and end apart: 42, of which 24 were waited for; matrix products, arithmetic and copies ran while one was open for 12% of the time, Pallas kernels for 10%

commit v1 on v0

--- a/solution.py
+++ b/solution.py
@@ -131,14 +131,22 @@
             else:
                 source, spot = ref.at[s], rows_both.at[s, :, pl.ds(i * height, height)]
             reads.append(pltpu.make_async_copy(source, spot, sem.at[s, i]))
-            pl.when(reach)(reads[-1].start)
+        if s % per == 0:
+            for i, t in enumerate(places):
+                k = (s // per) * len(places) + i
+                arrive.append(pltpu.make_async_copy(sources[k], pieces.at[k], piece_sem.at[k]))
+
+    def begin(s):
+        for read in reads[2 * s : 2 * s + 2]:
+            pl.when(reach)(read.start)
         if has_base:
             pl.when(extend)(nexts[s].start)
         if s % per == 0:
             for i, t in enumerate(places):
-                k = (s // per) * len(places) + i
-                arrive.append(pltpu.make_async_copy(sources[k], pieces.at[k], piece_sem.at[k]))
-                pl.when(upstream >= t)(arrive[-1].start)
+                pl.when(upstream >= t)(arrive[(s // per) * len(places) + i].start)
+
+    begin(0)
+    begin(1)
 
     def factor(s, start, count):
         if only is not None and raw:
@@ -163,6 +171,8 @@
             if s % per == 0:
                 for i, t in enumerate(places):
                     pl.when(upstream >= t)(arrive[first + i].wait)
+            if s + 2 < SNODES:
+                begin(s + 2)
             for i, t in enumerate(places):
                 if t == 0:
                     part[...] = jnp.dot(
@@ -347,7 +357,8 @@
         if n + 1 < HALVES:
             flows = [(got[s].pop(),) for s in range(STREAMS)]
         if n:
-            waiting = share_col(share_cores(total))
+            total = share_cores(total)
+            waiting = share_col(total)
         before = got
     if mine.ndim == 3:
         last_rows = [lax.dynamic_slice_in_dim(x, core * (nz - 1) * 2 * own_rows, 2 * own_rows, 2) for x in (mine, theirs)]
@@ -356,7 +367,7 @@
     back = lax.ppermute(
         after(jnp.concatenate(last_rows, axis=1), got[0][1]), "row", [(2 * nz - 2, 2 * nz - 4), (1, 3)]
     )
-    total = apply_update(table, after(meta, got[0][nz - 2]), mine, theirs, got, range(nz - 2), anc_blocks)
+    total = apply_update(table, after(meta, total), mine, theirs, got, range(nz - 2), anc_blocks)
     total = apply_update(table, after(meta, waiting), mine, theirs, got, [nz - 2], anc_blocks, total, back)
     total = jnp.concatenate([waiting, share_col(share_cores(total))], axis=-1)
     update = share_out(share_line(total))

time: 262 us -> 261 us (level)
    ppermute x2, starting transfers between devices: 17.4 us -> 12.3 us  [share_cores(): lax.ppermute(pick(total, 1 - core, 1), 'row', pair)]
    ppermute x3, waiting for transfers between devices: 6.33 us -> 2.97 us  [share_line(): lax.ppermute(pick(total, (z + d) % nz, 0), 'row', moves[d - 1])]
  transfers between devices with their start and end apart: 42 -> 42, of which waited for: 24 -> 22; matrix products, arithmetic and copies ran while one was open for 12% -> 12% of each run, Pallas kernels for 10% -> 10%
where the time goes in v1:
time: 261 us; the launch traced here: 260 us
  starting transfers between devices  109 us (42%)
  waiting for transfers between devices  68.6 us (26%)
  Pallas kernels  44.6 us (17%)
  other arithmetic  26.5 us (10%)
  local copies, waits for them, and re-layouts  9.47 us (4%)
    ppermute x18, starting transfers between devices, hop(): return lax.ppermute(value, 'row', up + down)  73.7 us
    ppermute x18, waiting for transfers between devices, hop(): return lax.ppermute(value, 'row', up + down)  49.1 us
    pallas_call x2, Pallas kernels, apply_product(): pl.pallas_call(functools.partial(product_kernel, first), in_specs=[pl.Blo...  27.8 us
    pallas_call x3, Pallas kernels, apply_update(): pl.pallas_call(functools.partial(update_kernel, places, has_base), out_sh...  16.8 us
    convert_element_type x6, other arithmetic, per_device(): (send.astype(F32) + jnp.where(upstream >= t - 1, 0.0, late)).astype(BF16)  14.5 us
    ppermute x2, starting transfers between devices, share_cores(): lax.ppermute(pick(total, 1 - core, 1), 'row', pair)  12.3 us
    ppermute x6, waiting for transfers between devices, share_col(): lax.ppermute(pick(total, col ^ d, 2), 'col', turns[d - 1])  10.7 us
    ppermute x6, starting transfers between devices, share_col(): lax.ppermute(pick(total, col ^ d, 2), 'col', turns[d - 1])  9.1 us
  transfers between devices with their start and end apart: 42, of which 22 were waited for; matrix products, arithmetic and copies ran while one was open for 12% of the time, Pallas kernels for 10%

profile of v1, /device:TPU:0, one launch (start us, length us, event | category | flops | bytes accessed | tf_op | source)
XLA Modules:
  0.0 259.8 jit_solution(6010410988767809879)
XLA Ops:
  1.3 13.7 %shard_map.77 = (bf16[3,2,512,384]{3,2,1,0:T(8,128)(2,1)}, bf16[4,2,512,384]{3,2,1,0:T(8,128)(2,1)}, bf16[3,2,512,384]{3,2,1,0:T(8,128)(2,1)}, bf16[4,2,512,384]{3,2,1,0:T(8,128)(2,1)}) custom-call(s32[3]{0:T(128)} %pad_add_fusion.meta_ref, bf16[4,4,512,1024]{3,2,1,0:T(8,128)(2,1)} %bitcast.144, bf16[4,1024,768]{2,1,0:T(8,128)(2,1)} %rhs_ref.3), custom_call_target="tpu_custom_call" | custom-call | flops 6442450944 | bytes 17825792 | tf_op jit(solution)/shard_map/pallas_call | solution.py:75
  15.5 14.1 %shard_map.78 = (bf16[3,2,512,384]{3,2,1,0:T(8,128)(2,1)}, bf16[4,2,512,384]{3,2,1,0:T(8,128)(2,1)}, bf16[3,2,512,384]{3,2,1,0:T(8,128)(2,1)}, bf16[4,2,512,384]{3,2,1,0:T(8,128)(2,1)}) custom-call(s32[3]{0:T(128)} %pad_add_fusion.meta_ref, bf16[4,4,512,1024]{3,2,1,0:T(8,128)(2,1)} %bitcast.145, bf16[4,1024,768]{2,1,0:T(8,128)(2,1)} %rhs_ref.3), custom_call_target="tpu_custom_call" | custom-call | flops 6442450944 | bytes 17825792 | tf_op jit(solution)/shard_map/pallas_call | solution.py:75
  29.9 4.9 %collective-permute-start.1 = (bf16[2,512,384]{2,1,0:T(8,128)(2,1)S(1)}, bf16[2,512,384]{2,1,0:T(8,128)(2,1)S(1)}, u32[]{:S(2)}, u32[]{:S(2)}) collective-permute-start(bf16[2,512,384]{2,1,0:T(8,128)(2,1)S(1)} %fusion.16), channel_id=1, source_target_pairs={{0,8},{28,20},{1,9},{29,21},{2,10},{30,22},{3,11},{31,23}} | collective-permute-start | bytes 2359304 | tf_op jit(solution)/shard_map/ppermute | solution.py:267
  34.9 1.4 fusion.17
  36.3 4.4 %collective-permute-start.12 = (bf16[2,512,384]{2,1,0:T(8,128)(2,1)S(1)}, bf16[2,512,384]{2,1,0:T(8,128)(2,1)S(1)}, u32[]{:S(2)}, u32[]{:S(2)}) collective-permute-start(bf16[2,512,384]{2,1,0:T(8,128)(2,1)S(1)} %fusion.17), channel_id=1, source_target_pairs={{0,8},{28,20},{1,9},{29,21},{2,10},{30,22},{3,11},{31,23}} | collective-permute-start | bytes 2359304 | tf_op jit(solution)/shard_map/ppermute | solution.py:267
  40.7 3.6 %collective-permute-done.1 = bf16[2,512,384]{2,1,0:T(8,128)(2,1)S(1)} collective-permute-done((bf16[2,512,384]{2,1,0:T(8,128)(2,1)S(1)}, bf16[2,512,384]{2,1,0:T(8,128)(2,1)S(1)}, u32[]{:S(2)}, u32[]{:S(2)}) %collective-permute-start.1) | collective-permute-done | bytes 786464 | tf_op jit(solution)/shard_map/ppermute | solution.py:267
  44.7 4.4 %collective-permute-start.2 = (bf16[2,512,384]{2,1,0:T(8,128)(2,1)S(1)}, bf16[2,512,384]{2,1,0:T(8,128)(2,1)S(1)}, u32[]{:S(2)}, u32[]{:S(2)}) collective-permute-start(bf16[2,512,384]{2,1,0:T(8,128)(2,1)S(1)} %fusion.12), channel_id=1, source_target_pairs={{0,8},{8,16},{28,20},{20,12},{1,9},{9,17},{29,21},{21,13},{2,10},{... | collective-permute-start | bytes 2359304 | tf_op jit(solution)/shard_map/ppermute | solution.py:267
  49.1 3.7 %collective-permute-done.12 = bf16[2,512,384]{2,1,0:T(8,128)(2,1)S(1)} collective-permute-done((bf16[2,512,384]{2,1,0:T(8,128)(2,1)S(1)}, bf16[2,512,384]{2,1,0:T(8,128)(2,1)S(1)}, u32[]{:S(2)}, u32[]{:S(2)}) %collective-permute-start.12) | collective-permute-done | bytes 786464 | tf_op jit(solution)/shard_map/ppermute | solution.py:267
  53.1 4.4 %collective-permute-start.13 = (bf16[2,512,384]{2,1,0:T(8,128)(2,1)S(1)}, bf16[2,512,384]{2,1,0:T(8,128)(2,1)S(1)}, u32[]{:S(2)}, u32[]{:S(2)}) collective-permute-start(bf16[2,512,384]{2,1,0:T(8,128)(2,1)S(1)} %fusion.7), channel_id=1, source_target_pairs={{0,8},{8,16},{28,20},{20,12},{1,9},{9,17},{29,21},{21,13},{2,10},{... | collective-permute-start | bytes 2359304 | tf_op jit(solution)/shard_map/ppermute | solution.py:267
  57.5 3.7 %collective-permute-done.2 = bf16[2,512,384]{2,1,0:T(8,128)(2,1)S(1)} collective-permute-done((bf16[2,512,384]{2,1,0:T(8,128)(2,1)S(1)}, bf16[2,512,384]{2,1,0:T(8,128)(2,1)S(1)}, u32[]{:S(2)}, u32[]{:S(2)}) %collective-permute-start.2) | collective-permute-done | bytes 786464 | tf_op jit(solution)/shard_map/ppermute | solution.py:267
  61.5 4.4 %collective-permute-start.3 = (bf16[2,512,384]{2,1,0:T(8,128)(2,1)S(1)}, bf16[2,512,384]{2,1,0:T(8,128)(2,1)S(1)}, u32[]{:S(2)}, u32[]{:S(2)}) collective-permute-start(bf16[2,512,384]{2,1,0:T(8,128)(2,1)S(1)} %fusion.13), channel_id=1, source_target_pairs={{0,8},{8,16},{16,24},{28,20},{20,12},{12,4},{1,9},{9,17},{17,25},{... | collective-permute-start | bytes 2359304 | tf_op jit(solution)/shard_map/ppermute | solution.py:267
  66.0 3.6 %collective-permute-done.13 = bf16[2,512,384]{2,1,0:T(8,128)(2,1)S(1)} collective-permute-done((bf16[2,512,384]{2,1,0:T(8,128)(2,1)S(1)}, bf16[2,512,384]{2,1,0:T(8,128)(2,1)S(1)}, u32[]{:S(2)}, u32[]{:S(2)}) %collective-permute-start.13) | collective-permute-done | bytes 786464 | tf_op jit(solution)/shard_map/ppermute | solution.py:267
  69.9 4.4 %collective-permute-start.14 = (bf16[2,512,384]{2,1,0:T(8,128)(2,1)S(1)}, bf16[2,512,384]{2,1,0:T(8,128)(2,1)S(1)}, u32[]{:S(2)}, u32[]{:S(2)}) collective-permute-start(bf16[2,512,384]{2,1,0:T(8,128)(2,1)S(1)} %fusion.8), channel_id=1, source_target_pairs={{0,8},{8,16},{16,24},{28,20},{20,12},{12,4},{1,9},{9,17},{17,25},{... | collective-permute-start | bytes 2359304 | tf_op jit(solution)/shard_map/ppermute | solution.py:267
  74.4 3.7 %collective-permute-done.3 = bf16[2,512,384]{2,1,0:T(8,128)(2,1)S(1)} collective-permute-done((bf16[2,512,384]{2,1,0:T(8,128)(2,1)S(1)}, bf16[2,512,384]{2,1,0:T(8,128)(2,1)S(1)}, u32[]{:S(2)}, u32[]{:S(2)}) %collective-permute-start.3) | collective-permute-done | bytes 786464 | tf_op jit(solution)/shard_map/ppermute | solution.py:267
  78.8 7.7 %collective-permute-done.14 = bf16[2,512,384]{2,1,0:T(8,128)(2,1)S(1)} collective-permute-done((bf16[2,512,384]{2,1,0:T(8,128)(2,1)S(1)}, bf16[2,512,384]{2,1,0:T(8,128)(2,1)S(1)}, u32[]{:S(2)}, u32[]{:S(2)}) %collective-permute-start.14) | collective-permute-done | bytes 786464 | tf_op jit(solution)/shard_map/ppermute | solution.py:267
  87.0 4.4 %collective-permute-start.5 = (bf16[2,512,384]{2,1,0:T(8,128)(2,1)S(1)}, bf16[2,512,384]{2,1,0:T(8,128)(2,1)S(1)}, u32[]{:S(2)}, u32[]{:S(2)}) collective-permute-start(bf16[2,512,384]{2,1,0:T(8,128)(2,1)S(1)} %add_convert_fusion.4.refs_0_), channel_id=1, source_target_pairs={{0,8},{8,16},{16,24},{28,20},{20,12},{12,4},{1,9},{9,17},{17,25},{... | collective-permute-start | bytes 2359304 | tf_op jit(solution)/shard_map/ppermute | solution.py:267
  91.4 1.3 add_convert_fusion.1.refs_4_
  92.8 2.4 collective-permute-start.16
  95.2 5.7 %collective-permute-done.5.refs_1_ = bf16[2,512,384]{2,1,0:T(8,128)(2,1)S(1)} collective-permute-done((bf16[2,512,384]{2,1,0:T(8,128)(2,1)S(1)}, bf16[2,512,384]{2,1,0:T(8,128)(2,1)S(1)}, u32[]{:S(2)}, u32[]{:S(2)}) %collective-permute-start.5) | collective-permute-done | bytes 786464 | tf_op jit(solution)/shard_map/ppermute | solution.py:267
  100.9 2.9 %fusion.11 = bf16[2,512,384]{2,1,0:T(8,128)(2,1)} fusion(bf16[2,512,384]{2,1,0:T(8,128)(2,1)S(1)} %collective-permute-done.5.refs_1_, bf16[3,2,512,384]{3,2,1,0:T(8,128)(2,1)} %collective-permute-done.6, bf16[4,2,512,384]{3,2,1,0:T(8,128)(2,1)} %get-tuple-element.18, pred[]{:T(512)S(6)} %ge.12), kind=kLoop, calls=%fused_computation.25 | loop fusion | flops 2752512 | bytes 3145729 | tf_op jit(solution)/shard_map/convert_element_type | solution.py:349
  103.8 5.3 %collective-permute-start.7 = (bf16[2,512,384]{2,1,0:T(8,128)(2,1)}, bf16[2,512,384]{2,1,0:T(8,128)(2,1)}, u32[]{:S(2)}, u32[]{:S(2)}) collective-permute-start(bf16[2,512,384]{2,1,0:T(8,128)(2,1)} %fusion.11), channel_id=1, source_target_pairs={{0,8},{8,16},{16,24},{28,20},{20,12},{12,4},{1,9},{9,17},{17,25},{... | collective-permute-start | bytes 2359304 | tf_op jit(solution)/shard_map/ppermute | solution.py:267
  110.2 2.6 %fusion.6 = bf16[2,512,384]{2,1,0:T(8,128)(2,1)} fusion(bf16[2,512,384]{2,1,0:T(8,128)(2,1)S(1)} %collective-permute-done.16.refs_5_, bf16[3,2,512,384]{3,2,1,0:T(8,128)(2,1)} %collective-permute-done.17, bf16[4,2,512,384]{3,2,1,0:T(8,128)(2,1)} %get-tuple-element.23, pred[]{:T(512)S(6)} %ge.12), kind=kLoop, calls=%fused_computation.15 | loop fusion | flops 2752512 | bytes 3145729 | tf_op jit(solution)/shard_map/convert_element_type | solution.py:349
  112.8 5.5 %collective-permute-start.18 = (bf16[2,512,384]{2,1,0:T(8,128)(2,1)}, bf16[2,512,384]{2,1,0:T(8,128)(2,1)}, u32[]{:S(2)}, u32[]{:S(2)}) collective-permute-start(bf16[2,512,384]{2,1,0:T(8,128)(2,1)} %fusion.6), channel_id=1, source_target_pairs={{0,8},{8,16},{16,24},{28,20},{20,12},{12,4},{1,9},{9,17},{17,25},{... | collective-permute-start | bytes 2359304 | tf_op jit(solution)/shard_map/ppermute | solution.py:267
  118.3 2.8 %fusion.10 = bf16[2,512,384]{2,1,0:T(8,128)(2,1)} fusion(bf16[2,512,384]{2,1,0:T(8,128)(2,1)} %collective-permute-done.7.refs_2_, bf16[3,2,512,384]{3,2,1,0:T(8,128)(2,1)} %collective-permute-done.6, bf16[4,2,512,384]{3,2,1,0:T(8,128)(2,1)} %get-tuple-element.18, pred[]{:T(512)S(6)} %ge.13), kind=kLoop, calls=%fused_computation.23 | loop fusion | flops 2752512 | bytes 3145729 | tf_op jit(solution)/shard_map/convert_element_type | solution.py:349
  121.2 4.9 %collective-permute-start.8 = (bf16[2,512,384]{2,1,0:T(8,128)(2,1)}, bf16[2,512,384]{2,1,0:T(8,128)(2,1)}, u32[]{:S(2)}, u32[]{:S(2)}) collective-permute-start(bf16[2,512,384]{2,1,0:T(8,128)(2,1)} %fusion.10), channel_id=1, source_target_pairs={{0,8},{8,16},{16,24},{28,20},{20,12},{12,4},{1,9},{9,17},{17,25},{... | collective-permute-start | bytes 2359304 | tf_op jit(solution)/shard_map/ppermute | solution.py:267
  127.2 1.7 fusion.5
  129.0 4.4 %collective-permute-start.19 = (bf16[2,512,384]{2,1,0:T(8,128)(2,1)S(1)}, bf16[2,512,384]{2,1,0:T(8,128)(2,1)S(1)}, u32[]{:S(2)}, u32[]{:S(2)}) collective-permute-start(bf16[2,512,384]{2,1,0:T(8,128)(2,1)S(1)} %fusion.5), channel_id=1, source_target_pairs={{0,8},{8,16},{16,24},{28,20},{20,12},{12,4},{1,9},{9,17},{17,25},{... | collective-permute-start | bytes 2359304 | tf_op jit(solution)/shard_map/ppermute | solution.py:267
  133.4 2.3 collective-permute-done.8.refs_3_
  135.7 1.7 fusion.9
  137.4 4.4 %collective-permute-start.9 = (bf16[2,512,384]{2,1,0:T(8,128)(2,1)S(1)}, bf16[2,512,384]{2,1,0:T(8,128)(2,1)S(1)}, u32[]{:S(2)}, u32[]{:S(2)}) collective-permute-start(bf16[2,512,384]{2,1,0:T(8,128)(2,1)S(1)} %fusion.9), channel_id=1, source_target_pairs={{0,8},{8,16},{16,24},{28,20},{20,12},{12,4},{1,9},{9,17},{17,25},{... | collective-permute-start | bytes 2359304 | tf_op jit(solution)/shard_map/ppermute | solution.py:267
  141.8 2.1 collective-permute-done.19.refs_7_
  144.0 2.7 %fusion.4 = bf16[2,512,384]{2,1,0:T(8,128)(2,1)} fusion(bf16[2,512,384]{2,1,0:T(8,128)(2,1)S(1)} %collective-permute-done.19.refs_7_, bf16[3,2,512,384]{3,2,1,0:T(8,128)(2,1)} %collective-permute-done.17, bf16[4,2,512,384]{3,2,1,0:T(8,128)(2,1)S(1)} %copy-done.11, pred[]{:T(512)S(6)} %ge.14), kind=kLoop, calls=%fused_computation.11 | loop fusion | flops 2752512 | bytes 3145729 | tf_op jit(solution)/shard_map/convert_element_type | solution.py:349
  146.6 4.6 %collective-permute-start.20 = (bf16[2,512,384]{2,1,0:T(8,128)(2,1)}, bf16[2,512,384]{2,1,0:T(8,128)(2,1)S(1)}, u32[]{:S(2)}, u32[]{:S(2)}) collective-permute-start(bf16[2,512,384]{2,1,0:T(8,128)(2,1)} %fusion.4), channel_id=1, source_target_pairs={{0,8},{8,16},{16,24},{28,20},{20,12},{12,4},{1,9},{9,17},{17,25},{... | collective-permute-start | bytes 2359304 | tf_op jit(solution)/shard_map/ppermute | solution.py:267
  153.1 7.9 %collective-permute-done.20 = bf16[2,512,384]{2,1,0:T(8,128)(2,1)S(1)} collective-permute-done((bf16[2,512,384]{2,1,0:T(8,128)(2,1)}, bf16[2,512,384]{2,1,0:T(8,128)(2,1)S(1)}, u32[]{:S(2)}, u32[]{:S(2)}) %collective-permute-start.20) | collective-permute-done | bytes 786464 | tf_op jit(solution)/shard_map/ppermute | solution.py:267
  161.0 1.3 fusion
  162.6 4.3 %collective-permute-start.22 = (bf16[2,512,384]{2,1,0:T(8,128)(2,1)S(1)}, bf16[2,512,384]{2,1,0:T(8,128)(2,1)S(1)}, u32[]{:S(2)}, u32[]{:S(2)}) collective-permute-start(bf16[2,512,384]{2,1,0:T(8,128)(2,1)S(1)} %add_convert_fusion.3.refs_0_), channel_id=1, source_target_pairs={{0,8},{8,16},{16,24},{28,20},{20,12},{12,4},{1,9},{9,17},{17,25},{... | collective-permute-start | bytes 2359304 | tf_op jit(solution)/shard_map/ppermute | solution.py:267
  170.4 3.2 %collective-permute-start.28 = (bf16[2,512,384]{2,1,0:T(8,128)(2,1)S(1)}, bf16[2,512,384]{2,1,0:T(8,128)(2,1)}, u32[]{:S(2)}, u32[]{:S(2)}) collective-permute-start(bf16[2,512,384]{2,1,0:T(8,128)(2,1)S(1)} %add_convert_fusion.refs_2_), channel_id=1, source_target_pairs={{0,8},{8,16},{16,24},{28,20},{20,12},{12,4},{1,9},{9,17},{17,25},{... | collective-permute-start | bytes 2359304 | tf_op jit(solution)/shard_map/ppermute | solution.py:267
  173.6 2.7 %collective-permute-done.22.refs_1_ = bf16[2,512,384]{2,1,0:T(8,128)(2,1)S(1)} collective-permute-done((bf16[2,512,384]{2,1,0:T(8,128)(2,1)S(1)}, bf16[2,512,384]{2,1,0:T(8,128)(2,1)S(1)}, u32[]{:S(2)}, u32[]{:S(2)}) %collective-permute-start.22) | collective-permute-done | bytes 786464 | tf_op jit(solution)/shard_map/ppermute | solution.py:267
  177.3 1.9 collective-permute-start.29
  179.2 6.7 %shard_map.79 = bf16[56,32,384]{2,1,0:T(8,128)(2,1)} custom-call(s32[112]{0:T(128)} %pad_add_fusion.1.table_ref, s32[3]{0:T(128)} %pad_add_fusion.meta_ref, bf16[4,224,2048]{2,1,0:T(8,128)(2,1)} %mine_ref.5, bf16[4,224,2048]{2,1,0:T(8,128)(2,1)} %collective-permute-done.23.theirs_ref, bf16[2,512,384]{2,1,0:T(8,128)(2,1)} %copy-done.7, ...), custom_call_target="tpu_custom_call" | custom-call | flops 2818572288 | bytes 8716288 | tf_op jit(solution)/shard_map/pallas_call | solution.py:222
  185.9 1.5 constant_dynamic-slice_fusion.3
  188.3 7.7 %collective-permute-start.24 = (bf16[4,7,4,8,384]{4,3,1,0,2:T(8,128)(2,1)}, bf16[4,7,4,8,384]{4,3,1,0,2:T(8,128)(2,1)}, u32[]{:S(2)}, u32[]{:S(2)}) collective-permute-start(bf16[4,7,4,8,384]{4,3,1,0,2:T(8,128)(2,1)} %bitcast.135), channel_id=1, source_target_pairs={{0,4},{4,0},{8,12},{12,8},{16,20},{20,16},{24,28},{28,24},{1,5},{5... | collective-permute-start | bytes 2064392 | tf_op jit(solution)/shard_map/ppermute | solution.py:282
  196.0 1.6 collective-permute-start.30
  197.5 1.5 collective-permute-start.31
  199.1 1.3 fusion.15
  200.4 1.6 collective-permute-start.25
  202.0 1.5 collective-permute-start.26
  203.5 2.8 %collective-permute-done.25 = bf16[4,7,8,384]{3,2,1,0:T(8,128)(2,1)S(1)} collective-permute-done((bf16[4,7,8,384]{3,2,1,0:T(8,128)(2,1)S(1)}, bf16[4,7,8,384]{3,2,1,0:T(8,128)(2,1)S(1)}, u32[]{:S(2)}, u32[]{:S(2)}) %collective-permute-start.25) | collective-permute-done | bytes 172064 | tf_op jit(solution)/shard_map/ppermute | solution.py:287
  206.3 2.5 collective-permute-start.27
  208.7 6.4 %shard_map.80.refs_0_ = bf16[56,32,384]{2,1,0:T(8,128)(2,1)} custom-call(s32[112]{0:T(128)} %pad_add_fusion.1.table_ref, s32[3]{0:T(128)} %pad_add_fusion.meta_ref, bf16[4,224,2048]{2,1,0:T(8,128)(2,1)} %mine_ref.5, bf16[4,224,2048]{2,1,0:T(8,128)(2,1)} %collective-permute-done.23.theirs_ref, bf16[2,512,384]{2,1,0:T(8,128)(2,1)} %copy-done.3, ...), custom_call_target="tpu_custom_call" | custom-call | flops 1409286144 | bytes 8716288 | tf_op jit(solution)/shard_map/pallas_call | solution.py:222
  215.3 3.7 %shard_map.81 = bf16[56,32,384]{2,1,0:T(8,128)(2,1)} custom-call(s32[112]{0:T(128)} %pad_add_fusion.1.table_ref, s32[3]{0:T(128)} %pad_add_fusion.meta_ref, bf16[4,224,2048]{2,1,0:T(8,128)(2,1)} %mine_ref.5, bf16[4,224,2048]{2,1,0:T(8,128)(2,1)} %collective-permute-done.23.theirs_ref, bf16[56,32,384]{2,1,0:T(8,128)(2,1)} %shard_map.80.refs_0_, ...), custom_call_target="tpu_custom_call" | custom-call | flops 704643072 | bytes 8716288 | tf_op jit(solution)/shard_map/pallas_call | solution.py:222
  219.0 2.1 dynamic-slice_bitcast_fusion
  221.2 4.6 %collective-permute-start.32 = (bf16[4,7,4,8,384]{4,3,2,1,0:T(8,128)(2,1)}, bf16[4,7,4,8,384]{4,3,2,1,0:T(8,128)(2,1)S(1)}, u32[]{:S(2)}, u32[]{:S(2)}) collective-permute-start(bf16[4,7,4,8,384]{4,3,2,1,0:T(8,128)(2,1)} %dynamic-slice_bitcast_fusion), channel_id=1, source_target_pairs={{0,4},{4,0},{8,12},{12,8},{16,20},{20,16},{24,28},{28,24},{1,5},{5... | collective-permute-start | bytes 2064392 | tf_op jit(solution)/shard_map/ppermute | solution.py:282
  225.8 1.9 collective-permute-done.32
  228.0 1.6 collective-permute-start.33
  229.6 1.5 collective-permute-start.34
  231.7 3.6 %collective-permute-done.33 = bf16[4,7,8,384]{3,2,1,0:T(8,128)(2,1)S(1)} collective-permute-done((bf16[4,7,8,384]{3,2,1,0:T(8,128)(2,1)S(1)}, bf16[4,7,8,384]{3,2,1,0:T(8,128)(2,1)S(1)}, u32[]{:S(2)}, u32[]{:S(2)}) %collective-permute-start.33) | collective-permute-done | bytes 172064 | tf_op jit(solution)/shard_map/ppermute | solution.py:287
  235.3 4.3 %collective-permute-done.34 = bf16[4,7,8,384]{3,2,1,0:T(8,128)(2,1)S(1)} collective-permute-done((bf16[4,7,8,384]{3,2,1,0:T(8,128)(2,1)S(1)}, bf16[4,7,8,384]{3,2,1,0:T(8,128)(2,1)S(1)}, u32[]{:S(2)}, u32[]{:S(2)}) %collective-permute-start.34) | collective-permute-done | bytes 172064 | tf_op jit(solution)/shard_map/ppermute | solution.py:287
  241.0 3.1 %collective-permute-start.37 = (bf16[7,8,768]{2,1,0:T(8,128)(2,1)S(1)}, bf16[7,8,768]{2,1,0:T(8,128)(2,1)S(1)}, u32[]{:S(2)}, u32[]{:S(2)}) collective-permute-start(bf16[7,8,768]{2,1,0:T(8,128)(2,1)S(1)} %get-tuple-element.41), channel_id=1, source_target_pairs={{0,16},{4,20},{8,24},{12,28},{16,0},{20,4},{24,8},{28,12},{1,17},{... | collective-permute-start | bytes 258056 | tf_op jit(solution)/shard_map/ppermute | solution.py:293
  244.1 2.8 %collective-permute-start.38 = (bf16[7,8,768]{2,1,0:T(8,128)(2,1)S(1)}, bf16[7,8,768]{2,1,0:T(8,128)(2,1)S(1)}, u32[]{:S(2)}, u32[]{:S(2)}) collective-permute-start(bf16[7,8,768]{2,1,0:T(8,128)(2,1)S(1)} %get-tuple-element.42), channel_id=1, source_target_pairs={{0,24},{4,28},{8,0},{12,4},{16,8},{20,12},{24,16},{28,20},{1,25},{... | collective-permute-start | bytes 258056 | tf_op jit(solution)/shard_map/ppermute | solution.py:293
  247.0 3.0 %collective-permute-done.37 = bf16[7,8,768]{2,1,0:T(8,128)(2,1)S(1)} collective-permute-done((bf16[7,8,768]{2,1,0:T(8,128)(2,1)S(1)}, bf16[7,8,768]{2,1,0:T(8,128)(2,1)S(1)}, u32[]{:S(2)}, u32[]{:S(2)}) %collective-permute-start.37) | collective-permute-done | bytes 86048 | tf_op jit(solution)/shard_map/ppermute | solution.py:293
  253.4 1.4 collective-permute-start.41
  255.2 1.8 collective-permute-done.40
  257.0 1.8 collective-permute-done.41
  (117 shorter events, 20.9 us)
Async XLA Ops:
  15.0 14.8 %collective-permute-start = (bf16[3,2,512,384]{3,2,1,0:T(8,128)(2,1)}, bf16[3,2,512,384]{3,2,1,0:T(8,128)(2,1)S(1)}, u32[]{:S(2)}, u32[]{:S(2)}) collective-permute-start(bf16[3,2,512,384]{3,2,1,0:T(8,128)(2,1)} %get-tuple-element.17), channel_id=1, source_target_pairs={{0,4},{4,0},{8,12},{12,8},{16,20},{20,16},{24,28},{28,24},{1,5},{5... | collective-permute-start | bytes 7077896 | tf_op jit(solution)/shard_map/ppermute | solution.py:274
  15.5 14.3 %copy-start.10 = (bf16[4,2,512,384]{3,2,1,0:T(8,128)(2,1)S(1)}, bf16[4,2,512,384]{3,2,1,0:T(8,128)(2,1)}, u32[]{:S(2)}) copy-start(bf16[4,2,512,384]{3,2,1,0:T(8,128)(2,1)} %get-tuple-element.16) | copy-start | bytes 9437188
  29.6 5.3 %collective-permute-start.11 = (bf16[3,2,512,384]{3,2,1,0:T(8,128)(2,1)}, bf16[3,2,512,384]{3,2,1,0:T(8,128)(2,1)S(1)}, u32[]{:S(2)}, u32[]{:S(2)}) collective-permute-start(bf16[3,2,512,384]{3,2,1,0:T(8,128)(2,1)} %get-tuple-element.22), channel_id=1, source_target_pairs={{0,4},{4,0},{8,12},{12,8},{16,20},{20,16},{24,28},{28,24},{1,5},{5... | collective-permute-start | bytes 7077896 | tf_op jit(solution)/shard_map/ppermute | solution.py:274
  29.9 14.4 %collective-permute-start.1 = (bf16[2,512,384]{2,1,0:T(8,128)(2,1)S(1)}, bf16[2,512,384]{2,1,0:T(8,128)(2,1)S(1)}, u32[]{:S(2)}, u32[]{:S(2)}) collective-permute-start(bf16[2,512,384]{2,1,0:T(8,128)(2,1)S(1)} %fusion.16), channel_id=1, source_target_pairs={{0,8},{28,20},{1,9},{29,21},{2,10},{30,22},{3,11},{31,23}} | collective-permute-start | bytes 2359304 | tf_op jit(solution)/shard_map/ppermute | solution.py:267
  36.3 16.5 %copy-start.9 = (bf16[4,2,512,384]{3,2,1,0:T(8,128)(2,1)S(1)}, bf16[4,2,512,384]{3,2,1,0:T(8,128)(2,1)}, u32[]{:S(2)}) copy-start(bf16[4,2,512,384]{3,2,1,0:T(8,128)(2,1)} %get-tuple-element.21) | copy-start | bytes 9437188
  36.3 16.5 %collective-permute-start.12 = (bf16[2,512,384]{2,1,0:T(8,128)(2,1)S(1)}, bf16[2,512,384]{2,1,0:T(8,128)(2,1)S(1)}, u32[]{:S(2)}, u32[]{:S(2)}) collective-permute-start(bf16[2,512,384]{2,1,0:T(8,128)(2,1)S(1)} %fusion.17), channel_id=1, source_target_pairs={{0,8},{28,20},{1,9},{29,21},{2,10},{30,22},{3,11},{31,23}} | collective-permute-start | bytes 2359304 | tf_op jit(solution)/shard_map/ppermute | solution.py:267
  44.7 16.5 %collective-permute-start.2 = (bf16[2,512,384]{2,1,0:T(8,128)(2,1)S(1)}, bf16[2,512,384]{2,1,0:T(8,128)(2,1)S(1)}, u32[]{:S(2)}, u32[]{:S(2)}) collective-permute-start(bf16[2,512,384]{2,1,0:T(8,128)(2,1)S(1)} %fusion.12), channel_id=1, source_target_pairs={{0,8},{8,16},{28,20},{20,12},{1,9},{9,17},{29,21},{21,13},{2,10},{... | collective-permute-start | bytes 2359304 | tf_op jit(solution)/shard_map/ppermute | solution.py:267
  53.1 16.5 %collective-permute-start.13 = (bf16[2,512,384]{2,1,0:T(8,128)(2,1)S(1)}, bf16[2,512,384]{2,1,0:T(8,128)(2,1)S(1)}, u32[]{:S(2)}, u32[]{:S(2)}) collective-permute-start(bf16[2,512,384]{2,1,0:T(8,128)(2,1)S(1)} %fusion.7), channel_id=1, source_target_pairs={{0,8},{8,16},{28,20},{20,12},{1,9},{9,17},{29,21},{21,13},{2,10},{... | collective-permute-start | bytes 2359304 | tf_op jit(solution)/shard_map/ppermute | solution.py:267
  61.5 16.5 %collective-permute-start.3 = (bf16[2,512,384]{2,1,0:T(8,128)(2,1)S(1)}, bf16[2,512,384]{2,1,0:T(8,128)(2,1)S(1)}, u32[]{:S(2)}, u32[]{:S(2)}) collective-permute-start(bf16[2,512,384]{2,1,0:T(8,128)(2,1)S(1)} %fusion.13), channel_id=1, source_target_pairs={{0,8},{8,16},{16,24},{28,20},{20,12},{12,4},{1,9},{9,17},{17,25},{... | collective-permute-start | bytes 2359304 | tf_op jit(solution)/shard_map/ppermute | solution.py:267
  66.0 29.2 %collective-permute-start.6 = (bf16[3,2,512,384]{3,2,1,0:T(8,128)(2,1)}, bf16[3,2,512,384]{3,2,1,0:T(8,128)(2,1)}, u32[]{:S(2)}, u32[]{:S(2)}) collective-permute-start(bf16[3,2,512,384]{3,2,1,0:T(8,128)(2,1)} %get-tuple-element.19), channel_id=1, source_target_pairs={{0,4},{4,0},{8,12},{12,8},{16,20},{20,16},{24,28},{28,24},{1,5},{5... | collective-permute-start | bytes 7077896 | tf_op jit(solution)/shard_map/ppermute | solution.py:274
  69.9 16.5 %collective-permute-start.14 = (bf16[2,512,384]{2,1,0:T(8,128)(2,1)S(1)}, bf16[2,512,384]{2,1,0:T(8,128)(2,1)S(1)}, u32[]{:S(2)}, u32[]{:S(2)}) collective-permute-start(bf16[2,512,384]{2,1,0:T(8,128)(2,1)S(1)} %fusion.8), channel_id=1, source_target_pairs={{0,8},{8,16},{16,24},{28,20},{20,12},{12,4},{1,9},{9,17},{17,25},{... | collective-permute-start | bytes 2359304 | tf_op jit(solution)/shard_map/ppermute | solution.py:267
  78.2 8.5 %collective-permute-start.4 = (bf16[2,512,384]{2,1,0:T(8,128)(2,1)S(1)}, bf16[2,512,384]{2,1,0:T(8,128)(2,1)S(1)}, u32[]{:S(2)}, u32[]{:S(2)}) collective-permute-start(bf16[2,512,384]{2,1,0:T(8,128)(2,1)S(1)} %fusion.3), channel_id=1, source_target_pairs={{0,4},{4,0},{8,12},{12,8},{16,20},{20,16},{24,28},{28,24},{1,5},{5... | collective-permute-start | bytes 2359304 | tf_op jit(solution)/shard_map/ppermute | solution.py:339
  78.3 30.8 %collective-permute-start.17 = (bf16[3,2,512,384]{3,2,1,0:T(8,128)(2,1)}, bf16[3,2,512,384]{3,2,1,0:T(8,128)(2,1)}, u32[]{:S(2)}, u32[]{:S(2)}) collective-permute-start(bf16[3,2,512,384]{3,2,1,0:T(8,128)(2,1)} %get-tuple-element.24), channel_id=1, source_target_pairs={{0,4},{4,0},{8,12},{12,8},{16,20},{20,16},{24,28},{28,24},{1,5},{5... | collective-permute-start | bytes 7077896 | tf_op jit(solution)/shard_map/ppermute | solution.py:274
  86.7 4.8 %collective-permute-start.15 = (bf16[2,512,384]{2,1,0:T(8,128)(2,1)S(1)}, bf16[2,512,384]{2,1,0:T(8,128)(2,1)}, u32[]{:S(2)}, u32[]{:S(2)}) collective-permute-start(bf16[2,512,384]{2,1,0:T(8,128)(2,1)S(1)} %fusion.1), channel_id=1, source_target_pairs={{0,4},{4,0},{8,12},{12,8},{16,20},{20,16},{24,28},{28,24},{1,5},{5... | collective-permute-start | bytes 2359304 | tf_op jit(solution)/shard_map/ppermute | solution.py:339
  87.0 16.8 %copy-start.7 = (bf16[2,512,384]{2,1,0:T(8,128)(2,1)}, bf16[2,512,384]{2,1,0:T(8,128)(2,1)S(1)}, u32[]{:S(2)}) copy-start(bf16[2,512,384]{2,1,0:T(8,128)(2,1)S(1)} %add_convert_fusion.4.refs_0_) | copy-start | bytes 2359300
  87.0 13.9 %collective-permute-start.5 = (bf16[2,512,384]{2,1,0:T(8,128)(2,1)S(1)}, bf16[2,512,384]{2,1,0:T(8,128)(2,1)S(1)}, u32[]{:S(2)}, u32[]{:S(2)}) collective-permute-start(bf16[2,512,384]{2,1,0:T(8,128)(2,1)S(1)} %add_convert_fusion.4.refs_0_), channel_id=1, source_target_pairs={{0,8},{8,16},{16,24},{28,20},{20,12},{12,4},{1,9},{9,17},{17,25},{... | collective-permute-start | bytes 2359304 | tf_op jit(solution)/shard_map/ppermute | solution.py:267
  92.8 11.0 %copy-start.5 = (bf16[2,512,384]{2,1,0:T(8,128)(2,1)}, bf16[2,512,384]{2,1,0:T(8,128)(2,1)S(1)}, u32[]{:S(2)}) copy-start(bf16[2,512,384]{2,1,0:T(8,128)(2,1)S(1)} %add_convert_fusion.1.refs_4_) | copy-start | bytes 2359300
  92.8 16.5 %collective-permute-start.16 = (bf16[2,512,384]{2,1,0:T(8,128)(2,1)S(1)}, bf16[2,512,384]{2,1,0:T(8,128)(2,1)S(1)}, u32[]{:S(2)}, u32[]{:S(2)}) collective-permute-start(bf16[2,512,384]{2,1,0:T(8,128)(2,1)S(1)} %add_convert_fusion.1.refs_4_), channel_id=1, source_target_pairs={{0,8},{8,16},{16,24},{28,20},{20,12},{12,4},{1,9},{9,17},{17,25},{... | collective-permute-start | bytes 2359304 | tf_op jit(solution)/shard_map/ppermute | solution.py:267
  100.9 2.9 %copy-start.13 = (bf16[2,512,384]{2,1,0:T(8,128)(2,1)}, bf16[2,512,384]{2,1,0:T(8,128)(2,1)S(1)}, u32[]{:S(2)}) copy-start(bf16[2,512,384]{2,1,0:T(8,128)(2,1)S(1)} %collective-permute-done.5.refs_1_) | copy-start | bytes 2359300
  103.8 14.5 %collective-permute-start.7 = (bf16[2,512,384]{2,1,0:T(8,128)(2,1)}, bf16[2,512,384]{2,1,0:T(8,128)(2,1)}, u32[]{:S(2)}, u32[]{:S(2)}) collective-permute-start(bf16[2,512,384]{2,1,0:T(8,128)(2,1)} %fusion.11), channel_id=1, source_target_pairs={{0,8},{8,16},{16,24},{28,20},{20,12},{12,4},{1,9},{9,17},{17,25},{... | collective-permute-start | bytes 2359304 | tf_op jit(solution)/shard_map/ppermute | solution.py:267
  109.1 59.7 %collective-permute-start.23 = (bf16[4,224,2048]{2,1,0:T(8,128)(2,1)}, bf16[4,224,2048]{2,1,0:T(8,128)(2,1)}, u32[]{:S(2)}, u32[]{:S(2)}) collective-permute-start(bf16[4,224,2048]{2,1,0:T(8,128)(2,1)} %mine_ref.5), channel_id=1, source_target_pairs={{0,4},{4,0},{8,12},{12,8},{16,20},{20,16},{24,28},{28,24},{1,5},{5... | collective-permute-start | bytes 11010056 | tf_op jit(solution)/shard_map/ppermute | solution.py:332
  109.3 0.9 copy-start.14
  112.8 14.5 %copy-start.11 = (bf16[4,2,512,384]{3,2,1,0:T(8,128)(2,1)S(1)}, bf16[4,2,512,384]{3,2,1,0:T(8,128)(2,1)}, u32[]{:S(2)}) copy-start(bf16[4,2,512,384]{3,2,1,0:T(8,128)(2,1)} %get-tuple-element.23) | copy-start | bytes 9437188
  112.8 14.5 %collective-permute-start.18 = (bf16[2,512,384]{2,1,0:T(8,128)(2,1)}, bf16[2,512,384]{2,1,0:T(8,128)(2,1)}, u32[]{:S(2)}, u32[]{:S(2)}) collective-permute-start(bf16[2,512,384]{2,1,0:T(8,128)(2,1)} %fusion.6), channel_id=1, source_target_pairs={{0,8},{8,16},{16,24},{28,20},{20,12},{12,4},{1,9},{9,17},{17,25},{... | collective-permute-start | bytes 2359304 | tf_op jit(solution)/shard_map/ppermute | solution.py:267
  121.2 14.5 %collective-permute-start.8 = (bf16[2,512,384]{2,1,0:T(8,128)(2,1)}, bf16[2,512,384]{2,1,0:T(8,128)(2,1)}, u32[]{:S(2)}, u32[]{:S(2)}) collective-permute-start(bf16[2,512,384]{2,1,0:T(8,128)(2,1)} %fusion.10), channel_id=1, source_target_pairs={{0,8},{8,16},{16,24},{28,20},{20,12},{12,4},{1,9},{9,17},{17,25},{... | collective-permute-start | bytes 2359304 | tf_op jit(solution)/shard_map/ppermute | solution.py:267
  126.1 9.6 %copy-start.12 = (bf16[4,2,512,384]{3,2,1,0:T(8,128)(2,1)S(1)}, bf16[4,2,512,384]{3,2,1,0:T(8,128)(2,1)}, u32[]{:S(2)}) copy-start(bf16[4,2,512,384]{3,2,1,0:T(8,128)(2,1)} %get-tuple-element.18) | copy-start | bytes 9437188
  129.0 15.0 %collective-permute-start.19 = (bf16[2,512,384]{2,1,0:T(8,128)(2,1)S(1)}, bf16[2,512,384]{2,1,0:T(8,128)(2,1)S(1)}, u32[]{:S(2)}, u32[]{:S(2)}) collective-permute-start(bf16[2,512,384]{2,1,0:T(8,128)(2,1)S(1)} %fusion.5), channel_id=1, source_target_pairs={{0,8},{8,16},{16,24},{28,20},{20,12},{12,4},{1,9},{9,17},{17,25},{... | collective-permute-start | bytes 2359304 | tf_op jit(solution)/shard_map/ppermute | solution.py:267
  137.4 15.0 %collective-permute-start.9 = (bf16[2,512,384]{2,1,0:T(8,128)(2,1)S(1)}, bf16[2,512,384]{2,1,0:T(8,128)(2,1)S(1)}, u32[]{:S(2)}, u32[]{:S(2)}) collective-permute-start(bf16[2,512,384]{2,1,0:T(8,128)(2,1)S(1)} %fusion.9), channel_id=1, source_target_pairs={{0,8},{8,16},{16,24},{28,20},{20,12},{12,4},{1,9},{9,17},{17,25},{... | collective-permute-start | bytes 2359304 | tf_op jit(solution)/shard_map/ppermute | solution.py:267
  144.0 2.7 %copy-start.15 = (bf16[2,512,384]{2,1,0:T(8,128)(2,1)}, bf16[2,512,384]{2,1,0:T(8,128)(2,1)S(1)}, u32[]{:S(2)}) copy-start(bf16[2,512,384]{2,1,0:T(8,128)(2,1)S(1)} %collective-permute-done.19.refs_7_) | copy-start | bytes 2359300
  146.6 6.1 %copy-start.18 = (s32[56,4]{0,1:T(4,128)S(1)}, s32[56,4]{0,1:T(4,128)}, u32[]{:S(2)}) copy-start(s32[56,4]{0,1:T(4,128)} %param.11) | copy-start | bytes 2692
  146.6 6.1 %copy-start.19 = (s32[56,4,1]{0,2,1:T(1,128)S(1)}, s32[56,4,1]{0,2,1:T(1,128)}, u32[]{:S(2)}) copy-start(s32[56,4,1]{0,2,1:T(1,128)} %param.10) | copy-start | bytes 2692
  146.6 14.3 %collective-permute-start.20 = (bf16[2,512,384]{2,1,0:T(8,128)(2,1)}, bf16[2,512,384]{2,1,0:T(8,128)(2,1)S(1)}, u32[]{:S(2)}, u32[]{:S(2)}) collective-permute-start(bf16[2,512,384]{2,1,0:T(8,128)(2,1)} %fusion.4), channel_id=1, source_target_pairs={{0,8},{8,16},{16,24},{28,20},{20,12},{12,4},{1,9},{9,17},{17,25},{... | collective-permute-start | bytes 2359304 | tf_op jit(solution)/shard_map/ppermute | solution.py:267
  152.6 9.8 %collective-permute-start.10 = (bf16[2,512,384]{2,1,0:T(8,128)(2,1)S(1)}, bf16[2,512,384]{2,1,0:T(8,128)(2,1)S(1)}, u32[]{:S(2)}, u32[]{:S(2)}) collective-permute-start(bf16[2,512,384]{2,1,0:T(8,128)(2,1)S(1)} %fusion.2), channel_id=1, source_target_pairs={{0,4},{4,0},{8,12},{12,8},{16,20},{20,16},{24,28},{28,24},{1,5},{5... | collective-permute-start | bytes 2359304 | tf_op jit(solution)/shard_map/ppermute | solution.py:339
  162.3 7.9 %collective-permute-start.21 = (bf16[2,512,384]{2,1,0:T(8,128)(2,1)S(1)}, bf16[2,512,384]{2,1,0:T(8,128)(2,1)S(1)}, u32[]{:S(2)}, u32[]{:S(2)}) collective-permute-start(bf16[2,512,384]{2,1,0:T(8,128)(2,1)S(1)} %fusion), channel_id=1, source_target_pairs={{0,4},{4,0},{8,12},{12,8},{16,20},{20,16},{24,28},{28,24},{1,5},{5... | collective-permute-start | bytes 2359304 | tf_op jit(solution)/shard_map/ppermute | solution.py:339
  162.6 7.4 %copy-start.3 = (bf16[2,512,384]{2,1,0:T(8,128)(2,1)}, bf16[2,512,384]{2,1,0:T(8,128)(2,1)S(1)}, u32[]{:S(2)}) copy-start(bf16[2,512,384]{2,1,0:T(8,128)(2,1)S(1)} %add_convert_fusion.3.refs_0_) | copy-start | bytes 2359300
  162.6 13.8 %collective-permute-start.22 = (bf16[2,512,384]{2,1,0:T(8,128)(2,1)S(1)}, bf16[2,512,384]{2,1,0:T(8,128)(2,1)S(1)}, u32[]{:S(2)}, u32[]{:S(2)}) collective-permute-start(bf16[2,512,384]{2,1,0:T(8,128)(2,1)S(1)} %add_convert_fusion.3.refs_0_), channel_id=1, source_target_pairs={{0,8},{8,16},{16,24},{28,20},{20,12},{12,4},{1,9},{9,17},{17,25},{... | collective-permute-start | bytes 2359304 | tf_op jit(solution)/shard_map/ppermute | solution.py:267
  170.4 15.5 %copy-start.1 = (bf16[2,512,384]{2,1,0:T(8,128)(2,1)}, bf16[2,512,384]{2,1,0:T(8,128)(2,1)S(1)}, u32[]{:S(2)}) copy-start(bf16[2,512,384]{2,1,0:T(8,128)(2,1)S(1)} %add_convert_fusion.refs_2_) | copy-start | bytes 2359300
  170.4 27.1 %collective-permute-start.28 = (bf16[2,512,384]{2,1,0:T(8,128)(2,1)S(1)}, bf16[2,512,384]{2,1,0:T(8,128)(2,1)}, u32[]{:S(2)}, u32[]{:S(2)}) collective-permute-start(bf16[2,512,384]{2,1,0:T(8,128)(2,1)S(1)} %add_convert_fusion.refs_2_), channel_id=1, source_target_pairs={{0,8},{8,16},{16,24},{28,20},{20,12},{12,4},{1,9},{9,17},{17,25},{... | collective-permute-start | bytes 2359304 | tf_op jit(solution)/shard_map/ppermute | solution.py:267
  176.4 0.9 copy-start.16
  177.3 38.0 %collective-permute-start.29 = (bf16[4,448,512]{2,1,0:T(8,128)(2,1)S(1)}, bf16[4,448,512]{2,1,0:T(8,128)(2,1)}, u32[]{:S(2)}, u32[]{:S(2)}) collective-permute-start(bf16[4,448,512]{2,1,0:T(8,128)(2,1)S(1)} %pad_maximum_fusion), channel_id=1, source_target_pairs={{24,16},{4,12},{25,17},{5,13},{26,18},{6,14},{27,19},{7,15}} | collective-permute-start | bytes 5505032 | tf_op jit(solution)/shard_map/ppermute | solution.py:367
  188.3 10.8 %collective-permute-start.24 = (bf16[4,7,4,8,384]{4,3,1,0,2:T(8,128)(2,1)}, bf16[4,7,4,8,384]{4,3,1,0,2:T(8,128)(2,1)}, u32[]{:S(2)}, u32[]{:S(2)}) collective-permute-start(bf16[4,7,4,8,384]{4,3,1,0,2:T(8,128)(2,1)} %bitcast.135), channel_id=1, source_target_pairs={{0,4},{4,0},{8,12},{12,8},{16,20},{20,16},{24,28},{28,24},{1,5},{5... | collective-permute-start | bytes 2064392 | tf_op jit(solution)/shard_map/ppermute | solution.py:282
  196.0 19.3 %collective-permute-start.30 = (bf16[2,512,384]{2,1,0:T(8,128)(2,1)}, bf16[2,512,384]{2,1,0:T(8,128)(2,1)}, u32[]{:S(2)}, u32[]{:S(2)}) collective-permute-start(bf16[2,512,384]{2,1,0:T(8,128)(2,1)} %copy-done.16), channel_id=1, source_target_pairs={{8,16},{16,24},{20,12},{12,4},{9,17},{17,25},{21,13},{13,5},{10,18... | collective-permute-start | bytes 2359304 | tf_op jit(solution)/shard_map/ppermute | solution.py:267
  197.5 17.8 %collective-permute-start.31 = (bf16[2,512,384]{2,1,0:T(8,128)(2,1)}, bf16[2,512,384]{2,1,0:T(8,128)(2,1)}, u32[]{:S(2)}, u32[]{:S(2)}) collective-permute-start(bf16[2,512,384]{2,1,0:T(8,128)(2,1)} %collective-permute-done.28.refs_3_), channel_id=1, source_target_pairs={{8,16},{16,24},{20,12},{12,4},{9,17},{17,25},{21,13},{13,5},{10,18... | collective-permute-start | bytes 2359304 | tf_op jit(solution)/shard_map/ppermute | solution.py:267
  200.4 5.8 %collective-permute-start.25 = (bf16[4,7,8,384]{3,2,1,0:T(8,128)(2,1)S(1)}, bf16[4,7,8,384]{3,2,1,0:T(8,128)(2,1)S(1)}, u32[]{:S(2)}, u32[]{:S(2)}) collective-permute-start(bf16[4,7,8,384]{3,2,1,0:T(8,128)(2,1)S(1)} %get-tuple-element.37), channel_id=1, source_target_pairs={{0,1},{1,0},{2,3},{3,2},{4,5},{5,4},{6,7},{7,6},{8,9},{9,8},{10,11... | collective-permute-start | bytes 516104 | tf_op jit(solution)/shard_map/ppermute | solution.py:287
  202.0 13.1 %collective-permute-start.26 = (bf16[4,7,8,384]{3,2,1,0:T(8,128)(2,1)S(1)}, bf16[4,7,8,384]{3,2,1,0:T(8,128)(2,1)S(1)}, u32[]{:S(2)}, u32[]{:S(2)}) collective-permute-start(bf16[4,7,8,384]{3,2,1,0:T(8,128)(2,1)S(1)} %get-tuple-element.39), channel_id=1, source_target_pairs={{0,2},{1,3},{2,0},{3,1},{4,6},{5,7},{6,4},{7,5},{8,10},{9,11},{10,... | collective-permute-start | bytes 516104 | tf_op jit(solution)/shard_map/ppermute | solution.py:287
  206.3 8.9 %collective-permute-start.27 = (bf16[4,7,8,384]{3,2,1,0:T(8,128)(2,1)S(1)}, bf16[4,7,8,384]{3,2,1,0:T(8,128)(2,1)S(1)}, u32[]{:S(2)}, u32[]{:S(2)}) collective-permute-start(bf16[4,7,8,384]{3,2,1,0:T(8,128)(2,1)S(1)} %get-tuple-element.38), channel_id=1, source_target_pairs={{0,3},{1,2},{2,1},{3,0},{4,7},{5,6},{6,5},{7,4},{8,11},{9,10},{10,... | collective-permute-start | bytes 516104 | tf_op jit(solution)/shard_map/ppermute | solution.py:287
  215.3 10.4 %copy-start.8 = (bf16[2,512,384]{2,1,0:T(8,128)(2,1)S(1)}, bf16[2,512,384]{2,1,0:T(8,128)(2,1)}, u32[]{:S(2)}) copy-start(bf16[2,512,384]{2,1,0:T(8,128)(2,1)} %copy-done.7) | copy-start | bytes 2359300
  219.0 8.7 %copy-start = (bf16[56,32,384]{2,1,0:T(8,128)(2,1)S(1)}, bf16[56,32,384]{2,1,0:T(8,128)(2,1)}, u32[]{:S(2)}) copy-start(bf16[56,32,384]{2,1,0:T(8,128)(2,1)} %shard_map.81) | copy-start | bytes 4128772
  221.2 6.6 %collective-permute-start.32 = (bf16[4,7,4,8,384]{4,3,2,1,0:T(8,128)(2,1)}, bf16[4,7,4,8,384]{4,3,2,1,0:T(8,128)(2,1)S(1)}, u32[]{:S(2)}, u32[]{:S(2)}) collective-permute-start(bf16[4,7,4,8,384]{4,3,2,1,0:T(8,128)(2,1)} %dynamic-slice_bitcast_fusion), channel_id=1, source_target_pairs={{0,4},{4,0},{8,12},{12,8},{16,20},{20,16},{24,28},{28,24},{1,5},{5... | collective-permute-start | bytes 2064392 | tf_op jit(solution)/shard_map/ppermute | solution.py:282
  225.8 5.8 %copy-start.6 = (bf16[2,512,384]{2,1,0:T(8,128)(2,1)S(1)}, bf16[2,512,384]{2,1,0:T(8,128)(2,1)}, u32[]{:S(2)}) copy-start(bf16[2,512,384]{2,1,0:T(8,128)(2,1)} %copy-done.5) | copy-start | bytes 2359300
  225.8 5.8 %copy-start.4 = (bf16[2,512,384]{2,1,0:T(8,128)(2,1)S(1)}, bf16[2,512,384]{2,1,0:T(8,128)(2,1)}, u32[]{:S(2)}) copy-start(bf16[2,512,384]{2,1,0:T(8,128)(2,1)} %copy-done.3) | copy-start | bytes 2359300
  228.0 18.9 %copy-start.2 = (bf16[2,512,384]{2,1,0:T(8,128)(2,1)S(1)}, bf16[2,512,384]{2,1,0:T(8,128)(2,1)}, u32[]{:S(2)}) copy-start(bf16[2,512,384]{2,1,0:T(8,128)(2,1)} %copy-done.1) | copy-start | bytes 2359300
  228.0 7.3 %collective-permute-start.33 = (bf16[4,7,8,384]{3,2,1,0:T(8,128)(2,1)S(1)}, bf16[4,7,8,384]{3,2,1,0:T(8,128)(2,1)S(1)}, u32[]{:S(2)}, u32[]{:S(2)}) collective-permute-start(bf16[4,7,8,384]{3,2,1,0:T(8,128)(2,1)S(1)} %get-tuple-element.34), channel_id=1, source_target_pairs={{0,1},{1,0},{2,3},{3,2},{4,5},{5,4},{6,7},{7,6},{8,9},{9,8},{10,11... | collective-permute-start | bytes 516104 | tf_op jit(solution)/shard_map/ppermute | solution.py:287
  229.6 10.0 %collective-permute-start.34 = (bf16[4,7,8,384]{3,2,1,0:T(8,128)(2,1)S(1)}, bf16[4,7,8,384]{3,2,1,0:T(8,128)(2,1)S(1)}, u32[]{:S(2)}, u32[]{:S(2)}) collective-permute-start(bf16[4,7,8,384]{3,2,1,0:T(8,128)(2,1)S(1)} %get-tuple-element.36), channel_id=1, source_target_pairs={{0,2},{1,3},{2,0},{3,1},{4,6},{5,7},{6,4},{7,5},{8,10},{9,11},{10,... | collective-permute-start | bytes 516104 | tf_op jit(solution)/shard_map/ppermute | solution.py:287
  231.1 8.5 %collective-permute-start.35 = (bf16[4,7,8,384]{3,2,1,0:T(8,128)(2,1)S(1)}, bf16[4,7,8,384]{3,2,1,0:T(8,128)(2,1)S(1)}, u32[]{:S(2)}, u32[]{:S(2)}) collective-permute-start(bf16[4,7,8,384]{3,2,1,0:T(8,128)(2,1)S(1)} %get-tuple-element.35), channel_id=1, source_target_pairs={{0,3},{1,2},{2,1},{3,0},{4,7},{5,6},{6,5},{7,4},{8,11},{9,10},{10,... | collective-permute-start | bytes 516104 | tf_op jit(solution)/shard_map/ppermute | solution.py:287
  239.8 7.2 %collective-permute-start.36 = (bf16[7,8,768]{2,1,0:T(8,128)(2,1)S(1)}, bf16[7,8,768]{2,1,0:T(8,128)(2,1)S(1)}, u32[]{:S(2)}, u32[]{:S(2)}) collective-permute-start(bf16[7,8,768]{2,1,0:T(8,128)(2,1)S(1)} %get-tuple-element.40), channel_id=1, source_target_pairs={{0,8},{4,12},{8,16},{12,20},{16,24},{20,28},{24,0},{28,4},{1,9},{5... | collective-permute-start | bytes 258056 | tf_op jit(solution)/shard_map/ppermute | solution.py:293
  241.0 9.0 %collective-permute-start.37 = (bf16[7,8,768]{2,1,0:T(8,128)(2,1)S(1)}, bf16[7,8,768]{2,1,0:T(8,128)(2,1)S(1)}, u32[]{:S(2)}, u32[]{:S(2)}) collective-permute-start(bf16[7,8,768]{2,1,0:T(8,128)(2,1)S(1)} %get-tuple-element.41), channel_id=1, source_target_pairs={{0,16},{4,20},{8,24},{12,28},{16,0},{20,4},{24,8},{28,12},{1,17},{... | collective-permute-start | bytes 258056 | tf_op jit(solution)/shard_map/ppermute | solution.py:293
  244.1 5.9 %collective-permute-start.38 = (bf16[7,8,768]{2,1,0:T(8,128)(2,1)S(1)}, bf16[7,8,768]{2,1,0:T(8,128)(2,1)S(1)}, u32[]{:S(2)}, u32[]{:S(2)}) collective-permute-start(bf16[7,8,768]{2,1,0:T(8,128)(2,1)S(1)} %get-tuple-element.42), channel_id=1, source_target_pairs={{0,24},{4,28},{8,0},{12,4},{16,8},{20,12},{24,16},{28,20},{1,25},{... | collective-permute-start | bytes 258056 | tf_op jit(solution)/shard_map/ppermute | solution.py:293
  250.0 8.8 %copy-start.17 = (f32[224,768]{1,0:T(8,128)S(1)}, f32[224,768]{1,0:T(8,128)}, u32[]{:S(2)}) copy-start(f32[224,768]{1,0:T(8,128)} %param.9) | copy-start | bytes 2064388
  250.1 5.1 %collective-permute-start.39 = (bf16[7,8,768]{2,1,0:T(8,128)(2,1)S(1)}, bf16[7,8,768]{2,1,0:T(8,128)(2,1)S(1)}, u32[]{:S(2)}, u32[]{:S(2)}) collective-permute-start(bf16[7,8,768]{2,1,0:T(8,128)(2,1)S(1)} %get-tuple-element.31), channel_id=1, source_target_pairs={{0,1},{1,0},{2,3},{3,2},{4,5},{5,4},{6,7},{7,6},{8,9},{9,8},{10,11... | collective-permute-start | bytes 258056 | tf_op jit(solution)/shard_map/ppermute | solution.py:300
  252.5 4.5 %collective-permute-start.40 = (bf16[7,8,768]{2,1,0:T(8,128)(2,1)S(1)}, bf16[7,8,768]{2,1,0:T(8,128)(2,1)S(1)}, u32[]{:S(2)}, u32[]{:S(2)}) collective-permute-start(bf16[7,8,768]{2,1,0:T(8,128)(2,1)S(1)} %get-tuple-element.31), channel_id=1, source_target_pairs={{0,2},{1,3},{2,0},{3,1},{4,6},{5,7},{6,4},{7,5},{8,10},{9,11},{10,... | collective-permute-start | bytes 258056 | tf_op jit(solution)/shard_map/ppermute | solution.py:300
  253.4 5.4 %collective-permute-start.41 = (bf16[7,8,768]{2,1,0:T(8,128)(2,1)S(1)}, bf16[7,8,768]{2,1,0:T(8,128)(2,1)S(1)}, u32[]{:S(2)}, u32[]{:S(2)}) collective-permute-start(bf16[7,8,768]{2,1,0:T(8,128)(2,1)S(1)} %get-tuple-element.31), channel_id=1, source_target_pairs={{0,3},{1,2},{2,1},{3,0},{4,7},{5,6},{6,5},{7,4},{8,11},{9,10},{10,... | collective-permute-start | bytes 258056 | tf_op jit(solution)/shard_map/ppermute | solution.py:300
